TPU v7x, 256 devices: a whole 4x4x8 slice. The times are simulated.
256 devices in a mesh: ctx: 16 (over y, x_hi, core), exp: 16 (over z, x_lo).
Axes of the slice: x: 4 (x_hi: 2, x_lo: 2; x = x_hi * 2 + x_lo), y: 4, z: 8, core: 2. Of those that a mesh axis runs over, the one named last changes fastest.
Arguments:
- queries: bfloat16 [32768, 16, 128], P(('ctx', 'exp')), may hold values from -6 to 6
- key_tensor: bfloat16 [32768, 2, 128], P(('ctx', 'exp')), may hold values from -6 to 6
- value_tensor: bfloat16 [32768, 2, 128], P(('ctx', 'exp')), may hold values from -6 to 6
- out_grad: bfloat16 [32768, 16, 128], P(('ctx', 'exp')), may hold values from -120 to 120
- log_norm: float32 [32768, 16], P(('ctx', 'exp')), may hold values from 6.5 to 8
- out_dot: float32 [32768, 16], P(('ctx', 'exp')), may hold values from -1200 to 1200
- span_order: int32 [32], replicated, may hold values from 0 to 31, each once
- moe_input: bfloat16 [32768, 2048], P(('ctx', 'exp')), may hold values from -6 to 6
- moe_grad: bfloat16 [32768, 2048], P(('ctx', 'exp')), may hold values from -60 to 60
- expert_ids: int32 [32768, 8], P(('ctx', 'exp')), may hold values from 0 to 127, all different within a row; in each aligned block of 128 rows (0 to 127, 128 to 255, ...) at most 10 rows name the same one
- keep_mask: int32 [32768, 8], P(('ctx', 'exp')), may hold values 0 or 1
- route_weight: float32 [32768, 8], P(('ctx', 'exp')), may hold values from 0.03 to 0.5
- w_gate: bfloat16 [16, 2048, 768], P('exp'), may hold values from -0.125 to 0.125
- w_up: bfloat16 [16, 2048, 768], P('exp'), may hold values from -0.125 to 0.125
- w_down: bfloat16 [16, 768, 2048], P('exp'), may hold values from -0.21875 to 0.21875
Outputs:
- grad_queries: bfloat16 [32768, 16, 128], P(('ctx', 'exp'))
- grad_keys: bfloat16 [32768, 2, 128], P(('ctx', 'exp'))
- grad_values: bfloat16 [32768, 2, 128], P(('ctx', 'exp'))
- grad_moe_input: bfloat16 [32768, 2048], P(('ctx', 'exp'))
Inputs may be any that keep to these rules, and one draw needn't show every extreme that they name: `span_order`: each span number appears once. `expert_ids`: the 8 ids of a row differ; within the rows of one device (aligned blocks of 128 rows) no expert is named by more than 10 rows, a bound that some block reaches.
All inputs are finite; a program needn't handle non-finite values. No bound on the sum of `keep_mask` on one device may be relied on, other than what follows from the above.
Results may differ from a plain program's by a relative error of at most 0.0058.
Values may be sent and summed in bfloat16 or wider, within the bound.
No kernel may reach another device: no remote copies, remote signals or barrier semaphores. Data moves between devices by JAX's collectives and lax.ppermute only.
A program may use at most 128 MiB of HBM per device.

v0:
```python
import functools
import math

import jax
import jax.numpy as jnp
from jax import lax
from jax.experimental import pallas as pl
from jax.experimental.pallas import tpu as pltpu
from jax.sharding import PartitionSpec as P

SLOT = 10
LANES = 128
CHUNK = 256
LONG = 1024
MIB = 1024 * 1024
VMEM = pl.BlockSpec(memory_space=pltpu.VMEM)
SMEM = pl.BlockSpec(memory_space=pltpu.SMEM)
ANY = pl.BlockSpec(memory_space=pl.ANY)
F32 = jnp.float32
BF16 = jnp.bfloat16


def dot(left, right):
    return jnp.dot(left, right, preferred_element_type=F32)


def dot_rows(left, right):
    return lax.dot_general(left, right, (((1,), (1,)), ((), ())), preferred_element_type=F32)


def dot_cols(left, right):
    return lax.dot_general(left, right, (((0,), (0,)), ((), ())), preferred_element_type=F32)


def split3(array):
    high = array.astype(BF16)
    rest = array - high.astype(F32)
    middle = rest.astype(BF16)
    return high, middle, (rest - middle.astype(F32)).astype(BF16)


def attention_kernel(
    scale,
    kv_blocks,
    span_ref,
    q_own,
    q_got,
    d_own,
    d_got,
    stat_own,
    stat_got,
    *rest,
):
    kv_refs = rest[:kv_blocks]
    dq_own, dq_got, own_ref = rest[kv_blocks : kv_blocks + 3]
    part_refs = rest[kv_blocks + 3 : 2 * kv_blocks + 2]
    keys, values, keys_t, dk_acc, dv_acc, dq_acc, stat_acc = rest[2 * kv_blocks + 2 :]
    me = lax.axis_index("ctx")
    chip = me // 2
    core = me % 2
    slots = span_ref.shape[0]
    half = keys.shape[0] // slots
    width = q_own.shape[1]
    repeat = width // half

    def span_of(chip_index, core_index, upper):
        place = chip_index * 2 + core_index
        return span_ref[slots - 1 - place if upper else place]

    stats = jnp.concatenate([stat_own[...], stat_got[...]], axis=0)
    rows = stats.shape[1]
    wide = rows * repeat
    spread = (
        lax.broadcasted_iota(jnp.int32, (rows, wide), 1) // repeat
        == lax.broadcasted_iota(jnp.int32, (rows, wide), 0)
    ).astype(F32).astype(BF16)
    high, middle, low = split3(stats)
    lanes = dot(high, spread) + (dot(middle, spread) + dot(low, spread))
    count = stats.shape[0] // repeat
    lanes = lanes.reshape(count, repeat, wide)
    head = lax.broadcasted_iota(jnp.int32, lanes.shape, 1)
    lane_head = lax.broadcasted_iota(jnp.int32, lanes.shape, 2) % repeat
    stat_acc[...] = jnp.sum(jnp.where(head == lane_head, lanes, 0.0), axis=1)

    for block in range(kv_blocks):
        for part in range(8):
            span = span_of(chip ^ (2 * block + part // 4), part // 2 % 2, part % 2)
            at = pl.ds(pl.multiple_of(span * half, half), half)
            rows = kv_refs[block][part * half : (part + 1) * half, :]
            keys[at, :] = rows[:, :LANES]
            values[at, :] = rows[:, LANES:]
    chunks = keys.shape[0] // CHUNK
    for chunk in range(chunks):
        at = slice(chunk * CHUNK, (chunk + 1) * CHUNK)
        keys_t[:, at] = keys[at, :].T
    dk_acc[...] = jnp.zeros_like(dk_acc)
    dv_acc[...] = jnp.zeros_like(dv_acc)
    factor = scale / math.log(2.0)

    for index in range(4):
        upper = index % 2
        if index < 2:
            q_ref, d_ref, dq_ref, who = q_own, d_own, dq_own, core
        else:
            q_ref, d_ref, dq_ref, who = q_got, d_got, dq_got, 1 - core
        line = 2 * (index // 2)
        span = span_of(chip, who, upper)
        queries = q_ref[upper]
        grads = d_ref[upper]
        norm = stat_acc[line : line + 1, upper * width : (upper + 1) * width] * (1.0 / math.log(2.0))
        inner = stat_acc[line + 1 : line + 2, upper * width : (upper + 1) * width]
        dq_acc[...] = jnp.zeros_like(dq_acc)

        def one(start, count, masked):
            at = pl.ds(pl.multiple_of(start, CHUNK), count)
            scores = dot_rows(keys[at, :], queries)
            probs = jnp.exp2(scores * factor - norm)
            if masked:
                key_pos = start + lax.broadcasted_iota(jnp.int32, scores.shape, 0)
                query_pos = span * half + lax.broadcasted_iota(jnp.int32, scores.shape, 1) // repeat
                probs = jnp.where(key_pos <= query_pos, probs, 0.0)
            dprobs = dot_rows(values[at, :], grads)
            dscores = (probs * (dprobs - inner)).astype(BF16)
            dv_acc[at, :] += dot(probs.astype(BF16), grads)
            dk_acc[at, :] += dot(dscores, queries)
            dq_acc[...] += dot(keys_t[:, at], dscores)

        ahead = span * half
        lax.fori_loop(0, ahead // LONG, lambda i, none: (one(i * LONG, LONG, False), none)[1], 0)
        rest_start = ahead // LONG * LONG

        @pl.when(ahead - rest_start >= LONG // 2)
        def _():
            one(rest_start, LONG // 2, False)

        tail = ahead // (LONG // 2) * (LONG // 2)

        @pl.when(ahead - tail >= CHUNK)
        def _():
            one(tail, LONG // 2, True)

        @pl.when(ahead - tail < CHUNK)
        def _():
            one(tail, CHUNK, True)

        dq_ref[upper] = (dq_acc[...].T * scale).astype(BF16)

    for block in range(kv_blocks):
        for part in range(8):
            span = span_of(chip ^ (2 * block + part // 4), part // 2 % 2, part % 2)
            at = pl.ds(pl.multiple_of(span * half, half), half)
            rows = slice(part * half, (part + 1) * half)
            if block == 0:
                own_ref[rows, :LANES] = dk_acc[at, :] * scale
                own_ref[rows, LANES:] = dv_acc[at, :]
            else:
                part_refs[block - 1][rows, :LANES] = (dk_acc[at, :] * scale).astype(BF16)
                part_refs[block - 1][rows, LANES:] = dv_acc[at, :].astype(BF16)


def attention(span_order, q_own, q_got, d_own, d_got, stat_own, stat_got, kv_list, scale):
    blocks = len(kv_list)
    rows = kv_list[0].shape[0]
    total = blocks * rows
    spans, width, _ = q_own.shape
    part = jax.ShapeDtypeStruct((rows, 2 * LANES), BF16)
    return pl.pallas_call(
        functools.partial(attention_kernel, scale, blocks),
        out_shape=(
            jax.ShapeDtypeStruct(q_own.shape, BF16),
            jax.ShapeDtypeStruct(q_own.shape, BF16),
            jax.ShapeDtypeStruct((rows, 2 * LANES), F32),
        )
        + (part,) * (blocks - 1),
        in_specs=[SMEM] + [VMEM] * (6 + blocks),
        out_specs=(VMEM,) * (2 + blocks),
        scratch_shapes=[
            pltpu.VMEM((total, LANES), BF16),
            pltpu.VMEM((total, LANES), BF16),
            pltpu.VMEM((LANES, total), BF16),
            pltpu.VMEM((total, LANES), F32),
            pltpu.VMEM((total, LANES), F32),
            pltpu.VMEM((LANES, width), F32),
            pltpu.VMEM((4, spans * width), F32),
        ],
        compiler_params=pltpu.CompilerParams(vmem_limit_bytes=16 * MIB),
        cost_estimate=pl.CostEstimate(
            flops=6 * spans * width * total * LANES * 2,
            bytes_accessed=6 * 1024 * 1024,
            transcendentals=spans * width * total // 12,
        ),
        name="attention",
    )(span_order, q_own, q_got, d_own, d_got, stat_own, stat_got, *kv_list)


def slots_to_chunks(tiles, experts, blocks, chunk_ref, first):
    for expert in range(experts):
        for block in range(blocks):
            at = first + block * SLOT
            chunk_ref[expert, at : at + SLOT, :] = tiles[block, expert * SLOT : (expert + 1) * SLOT, :]


def dispatch_kernel(ids_ref, keep_ref, weight_ref, x_hbm, g_hbm, send_ref, combine_ref, x_ref, g_ref, tiles, chunks, sems):
    loads = [
        pltpu.make_async_copy(source, target, sems.at[i])
        for i, (source, target) in enumerate(((x_hbm, x_ref), (g_hbm, g_ref)))
    ]
    for load in loads:
        load.start()
    top, rows = ids_ref.shape
    experts = send_ref.shape[0]
    blocks = x_ref.shape[1] // LANES
    slots = experts * SLOT
    line = lax.broadcasted_iota(jnp.int32, (slots, rows), 0)
    expert_of = line // SLOT
    slot_of = line - expert_of * SLOT
    ids = jnp.where(keep_ref[...] == 1, ids_ref[...], -1)
    weights = weight_ref[...]
    hit = jnp.zeros((slots, rows), F32)
    weight = jnp.zeros((slots, rows), F32)
    for k in range(top):
        match = ids[k : k + 1, :] == expert_of
        hit = jnp.where(match, 1.0, hit)
        weight = jnp.where(match, weights[k : k + 1, :], weight)
    earlier = (
        lax.broadcasted_iota(jnp.int32, (rows, rows), 0)
        < lax.broadcasted_iota(jnp.int32, (rows, rows), 1)
    ).astype(F32).astype(BF16)
    rank = dot(hit.astype(BF16), earlier)
    chosen = jnp.where(rank == slot_of.astype(F32), hit, 0.0)
    combine_ref[...] = chosen * weight
    pick = chosen.astype(BF16)
    for load, source, first in ((loads[0], x_ref, 0), (loads[1], g_ref, blocks * SLOT)):
        load.wait()
        for pair in range(blocks // 2):
            both = dot(pick, source[:, pair * 2 * LANES : (pair + 1) * 2 * LANES])
            tiles[2 * pair] = both[:, :LANES]
            tiles[2 * pair + 1] = both[:, LANES:]
        slots_to_chunks(tiles, experts, blocks, chunks, first)
    send_ref[...] = chunks[...].astype(BF16)


def dispatch(ids, keep, weight, x, g, experts):
    rows = ids.shape[0]
    blocks = x.shape[1] // LANES
    slots = experts * SLOT
    return pl.pallas_call(
        dispatch_kernel,
        out_shape=(
            jax.ShapeDtypeStruct((experts, 2 * blocks * SLOT, LANES), BF16),
            jax.ShapeDtypeStruct((slots, rows), F32),
        ),
        in_specs=[VMEM] * 3 + [ANY] * 2,
        out_specs=(VMEM, VMEM),
        scratch_shapes=[
            pltpu.VMEM(x.shape, BF16),
            pltpu.VMEM(g.shape, BF16),
            pltpu.VMEM((blocks, slots, LANES), F32),
            pltpu.VMEM((experts, 2 * blocks * SLOT, LANES), F32),
            pltpu.SemaphoreType.DMA((2,)),
        ],
        compiler_params=pltpu.CompilerParams(vmem_limit_bytes=60 * MIB),
        name="dispatch",
    )(ids.T, keep.T, weight.T, x, g)


def mlp_kernel(in_ref, *rest):
    weights_hbm = rest[:3]
    out_ref = rest[3]
    weights = rest[4:7]
    chunks, tiles, x_rows, g_rows, sems = rest[7:]
    sources = in_ref.shape[0]
    blocks = x_rows.shape[1] // LANES
    hidden = weights[0].shape[1]
    tile = 256
    loads = []
    for step in range(hidden // tile):
        part = slice(step * tile, (step + 1) * tile)
        for i in range(3):
            at = (slice(None), part) if i < 2 else (part, slice(None))
            load = pltpu.make_async_copy(weights_hbm[i].at[(0,) + at], weights[i].at[at], sems.at[3 * step + i])
            load.start()
            loads.append(load)
    chunks[...] = in_ref[...].astype(F32)
    for rows_ref, first in ((x_rows, 0), (g_rows, blocks * SLOT)):
        for block in range(blocks):
            for source in range(sources):
                at = first + block * SLOT
                tiles[block, source * SLOT : (source + 1) * SLOT, :] = chunks[source, at : at + SLOT, :]
            rows_ref[:, block * LANES : (block + 1) * LANES] = tiles[block].astype(BF16)
    total = None
    for step in range(hidden // tile):
        for i in range(3):
            loads[3 * step + i].wait()
        part = slice(step * tile, (step + 1) * tile)
        gate_w, up_w = weights[0][:, part], weights[1][:, part]
        gate_pre = dot(x_rows[...], gate_w)
        up_pre = dot(x_rows[...], up_w)
        hidden_grad = dot_rows(g_rows[...], weights[2][part, :])
        sig = jax.nn.sigmoid(gate_pre)
        gate_grad = (hidden_grad * up_pre * sig * (1.0 + gate_pre * (1.0 - sig))).astype(BF16)
        up_grad = (hidden_grad * gate_pre * sig).astype(BF16)
        term = dot_rows(gate_grad, gate_w) + dot_rows(up_grad, up_w)
        for block in range(blocks):
            piece = term[:, block * LANES : (block + 1) * LANES]
            tiles[block] = piece if step == 0 else tiles[block] + piece
    slots_to_chunks(tiles, sources, blocks, chunks, 0)
    out_ref[...] = chunks[:, : blocks * SLOT, :].astype(BF16)


def mlp(received, w_gate, w_up, w_down):
    sources, chunk_rows, _ = received.shape
    _, width, hidden = w_gate.shape
    blocks = width // LANES
    slots = sources * SLOT
    return pl.pallas_call(
        mlp_kernel,
        out_shape=jax.ShapeDtypeStruct((sources, blocks * SLOT, LANES), BF16),
        in_specs=[VMEM] + [ANY] * 3,
        out_specs=VMEM,
        scratch_shapes=[
            pltpu.VMEM((width, hidden), BF16),
            pltpu.VMEM((width, hidden), BF16),
            pltpu.VMEM((hidden, width), BF16),
            pltpu.VMEM((sources, chunk_rows, LANES), F32),
            pltpu.VMEM((blocks, slots, LANES), F32),
            pltpu.VMEM((slots, width), BF16),
            pltpu.VMEM((slots, width), BF16),
            pltpu.SemaphoreType.DMA((9,)),
        ],
        compiler_params=pltpu.CompilerParams(vmem_limit_bytes=58 * MIB),
        cost_estimate=pl.CostEstimate(
            flops=10 * slots * width * hidden, bytes_accessed=11 * 1024 * 1024, transcendentals=slots * hidden
        ),
        name="experts",
    )(received, w_gate, w_up, w_down)


def combine_kernel(weight_ref, back_ref, out_ref, chunks, tiles):
    experts = back_ref.shape[0]
    blocks = out_ref.shape[1] // LANES
    chunks[...] = back_ref[...].astype(F32)
    weight = weight_ref[...].T
    high = weight.astype(BF16)
    rest = weight - high.astype(F32)
    middle = rest.astype(BF16)
    low = (rest - middle.astype(F32)).astype(BF16)
    for block in range(blocks):
        for expert in range(experts):
            at = block * SLOT
            tiles[block, expert * SLOT : (expert + 1) * SLOT, :] = chunks[expert, at : at + SLOT, :]
    for pair in range(blocks // 2):
        rows = jnp.concatenate([tiles[2 * pair], tiles[2 * pair + 1]], axis=1).astype(BF16)
        out = dot(high, rows) + (dot(middle, rows) + dot(low, rows))
        out_ref[:, pair * 2 * LANES : (pair + 1) * 2 * LANES] = out.astype(BF16)


def combine(weight, back):
    experts, chunk_rows, _ = back.shape
    slots, rows = weight.shape
    blocks = chunk_rows // SLOT
    return pl.pallas_call(
        combine_kernel,
        out_shape=jax.ShapeDtypeStruct((rows, blocks * LANES), BF16),
        in_specs=[VMEM, VMEM],
        out_specs=VMEM,
        scratch_shapes=[
            pltpu.VMEM((experts, chunk_rows, LANES), F32),
            pltpu.VMEM((blocks, slots, LANES), F32),
        ],
        compiler_params=pltpu.CompilerParams(vmem_limit_bytes=12 * MIB),
        name="combine",
    )(weight, back)


def on_device(
    queries,
    key_tensor,
    value_tensor,
    out_grad,
    log_norm,
    out_dot,
    span_order,
    moe_input,
    moe_grad,
    expert_ids,
    keep_mask,
    route_weight,
    w_gate,
    w_up,
    w_down,
):
    rows, heads, size = queries.shape
    group = heads // 2
    scale = 1.0 / math.sqrt(size)
    members = lax.axis_size("ctx")
    experts = lax.axis_size("exp")
    first = lax.axis_index("ctx") & 1 == 0
    chips = members // 2
    trade = lambda array, k: lax.ppermute(array, "ctx", [(i, i ^ k) for i in range(members)])

    send, weight = dispatch(expert_ids, keep_mask, route_weight, moe_input, moe_grad, experts)
    send, key_tensor, value_tensor = lax.optimization_barrier((send, key_tensor, value_tensor))
    kv = jnp.concatenate([key_tensor, value_tensor], axis=2)
    kv_own = jnp.where(first, kv[:, 0], kv[:, 1])
    kv_away = jnp.where(first, kv[:, 1], kv[:, 0])
    kv_got = trade(kv_away, 1)
    kv_near, kv_cross = trade(kv_own, 2), trade(kv_away, 3)
    ordered = lambda mine, other: [jnp.where(first, mine, other), jnp.where(first, other, mine)]
    kv_pair = jnp.concatenate(ordered(kv_own, kv_got) + ordered(kv_near, kv_cross), axis=0)
    received = lax.all_to_all(send, "exp", split_axis=0, concat_axis=0, tiled=True)
    kv_list = [kv_pair] + [trade(kv_pair, 4 * k) for k in range(1, chips // 2)]

    kv_near, queries, out_grad, log_norm, out_dot = lax.optimization_barrier(
        (kv_near, queries, out_grad, log_norm, out_dot)
    )

    def halves(array, axis):
        low, high = jnp.split(array, 2, axis=axis)
        return jnp.where(first, low, high), jnp.where(first, high, low)

    q_own, q_away = halves(queries, 1)
    d_own, d_away = halves(out_grad, 1)
    stat_own, stat_away = halves(jnp.stack([log_norm.T, out_dot.T]), 1)
    q_got, d_got = trade(q_away, 1), trade(d_away, 1)
    stat_got = trade(stat_away, 1)

    spans = lambda array: array.reshape(2, rows // 2 * group, size)
    dq_own, dq_got, own_sum, *parts = attention(
        span_order,
        spans(q_own),
        spans(q_got),
        spans(d_own),
        spans(d_got),
        stat_own.reshape(2 * group, rows),
        stat_got.reshape(2 * group, rows),
        kv_list,
        scale,
    )
    received, _ = lax.optimization_barrier((received, parts[0]))
    slot_grad = mlp(received, w_gate, w_up, w_down)
    returned = lax.all_to_all(slot_grad, "exp", split_axis=0, concat_axis=0, tiled=True)

    total, _ = lax.optimization_barrier((own_sum, slot_grad))
    for k in range(1, chips // 2):
        total = total + trade(parts[k - 1], 4 * k).astype(F32)
    blocks = [total[i * rows : (i + 1) * rows] for i in range(4)]
    mine, near = ordered(blocks[0], blocks[1]), ordered(blocks[2], blocks[3])
    own_head = mine[0] + trade(near[0].astype(BF16), 2).astype(F32)
    other_head = trade(mine[1].astype(BF16), 1).astype(F32) + trade(near[1].astype(BF16), 3).astype(F32)
    dq_got, _ = lax.optimization_barrier((dq_got, slot_grad))
    dq_back = trade(dq_got, 1)

    def joined(own, other):
        return jnp.concatenate(ordered(own, other), axis=1)

    grad_queries = joined(dq_own.reshape(rows, group, size), dq_back.reshape(rows, group, size))
    kv_grads = joined(own_head.astype(BF16)[:, None, :], other_head.astype(BF16)[:, None, :])
    grad_moe = combine(weight, returned)
    return grad_queries, kv_grads[:, :, :size], kv_grads[:, :, size:], grad_moe


def solution(mesh):
    rows = P(("ctx", "exp"))
    in_specs = (rows,) * 6 + (P(),) + (rows,) * 5 + (P("exp"),) * 3
    return jax.shard_map(
        on_device, mesh=mesh, in_specs=in_specs, out_specs=(rows,) * 4, check_vma=False
    )
```

profile of v0, /device:TPU:8, one launch (start us, length us, event | category | flops | bytes accessed | tf_op | source)
XLA Modules:
  0.0 91.7 jit_solution(7358004101112402179)
XLA Ops:
  0.6 0.0 copy-start.5
  0.6 0.0 copy-start.4
  0.7 0.0 copy-start.6
  0.7 0.0 copy-start.7
  0.7 0.0 copy-start.2
  0.7 0.0 copy-start.3
  0.7 4.0 %dispatch.1 = (bf16[16,320,128]{2,1,0:T(8,128)(2,1)}, f32[160,128]{1,0:T(8,128)}) custom-call(s32[8,128]{1,0:T(8,128)} %bitcast.36, s32[8,128]{1,0:T(8,128)} %bitcast.37, f32[8,128]{1,0:T(8,128)} %bitcast.38, bf16[128,2048]{1,0:T(8,128)(2,1)} %x_hbm.1, bf16[128,2048]{1,0:T(8,128)(2,1)} %g_hbm.1), custom_call_target="tpu_custom_call" | custom-call | tf_op jit(solution)/shard_map/dispatch/pallas_call | solution.py:247
  4.7 0.0 copy-start.1
  4.7 9.5 %all-to-all-start = ((bf16[16,320,128]{2,1,0:T(8,128)(2,1)}), bf16[16,320,128]{2,1,0:T(8,128)(2,1)}, u32[]{:S(2)}, u32[]{:S(2)}) async-start(bf16[16,320,128]{2,1,0:T(8,128)(2,1)} %get-tuple-element.31), calls=%async_computation | async-start | bytes 2621440 | tf_op jit(solution)/shard_map/all_to_all | solution.py:411
  14.2 0.0 copy-done.4
  14.3 0.0 copy-done.5
  14.3 0.1 collective-permute-start.4
  14.4 2.9 %collective-permute-start.5 = (bf16[128,256]{1,0:T(8,128)(2,1)S(1)}, bf16[128,256]{1,0:T(8,128)(2,1)S(1)}, u32[]{:S(2)}, u32[]{:S(2)}) collective-permute-start(bf16[128,256]{1,0:T(8,128)(2,1)S(1)} %select_bitcast_fusion.2), channel_id=1, source_target_pairs={{0,48},{16,32},{32,16},{48,0},{64,112},{80,96},{96,80},{112,64},{1... | collective-permute-start | bytes 196616 | tf_op jit(solution)/shard_map/ppermute | solution.py:400
  17.3 0.0 collective-permute-done.4
  17.3 1.2 %collective-permute-start = (bf16[128,256]{1,0:T(8,128)(2,1)S(1)}, bf16[128,256]{1,0:T(8,128)(2,1)S(1)}, u32[]{:S(2)}, u32[]{:S(2)}) collective-permute-start(bf16[128,256]{1,0:T(8,128)(2,1)S(1)} %get-tuple-element.47), channel_id=1, source_target_pairs={{0,32},{16,48},{32,0},{48,16},{64,96},{80,112},{96,64},{112,80},{1... | collective-permute-start | bytes 196616 | tf_op jit(solution)/shard_map/ppermute | solution.py:400
  18.5 1.8 %collective-permute-done.5 = bf16[128,256]{1,0:T(8,128)(2,1)S(1)} collective-permute-done((bf16[128,256]{1,0:T(8,128)(2,1)S(1)}, bf16[128,256]{1,0:T(8,128)(2,1)S(1)}, u32[]{:S(2)}, u32[]{:S(2)}) %collective-permute-start.5) | collective-permute-done | bytes 65568 | tf_op jit(solution)/shard_map/ppermute | solution.py:400
  20.3 2.8 %collective-permute-done = bf16[128,256]{1,0:T(8,128)(2,1)S(1)} collective-permute-done((bf16[128,256]{1,0:T(8,128)(2,1)S(1)}, bf16[128,256]{1,0:T(8,128)(2,1)S(1)}, u32[]{:S(2)}, u32[]{:S(2)}) %collective-permute-start) | collective-permute-done | bytes 65568 | tf_op jit(solution)/shard_map/ppermute | solution.py:400
  23.2 1.7 %collective-permute-start.8 = (bf16[512,256]{1,0:T(8,128)(2,1)S(1)}, bf16[512,256]{1,0:T(8,128)(2,1)S(1)}, u32[]{:S(2)}, u32[]{:S(2)}) collective-permute-start(bf16[512,256]{1,0:T(8,128)(2,1)S(1)} %pad_maximum_fusion.1.rest_0_), channel_id=1, source_target_pairs={{0,192},{16,208},{32,224},{48,240},{64,128},{80,144},{96,160},{112... | collective-permute-start | bytes 786440 | tf_op jit(solution)/shard_map/ppermute | solution.py:400
  24.9 0.9 %collective-permute-start.7 = (bf16[512,256]{1,0:T(8,128)(2,1)S(1)}, bf16[512,256]{1,0:T(8,128)(2,1)S(1)}, u32[]{:S(2)}, u32[]{:S(2)}) collective-permute-start(bf16[512,256]{1,0:T(8,128)(2,1)S(1)} %pad_maximum_fusion.1.rest_0_), channel_id=1, source_target_pairs={{0,128},{16,144},{32,160},{48,176},{64,192},{80,208},{96,224},{112... | collective-permute-start | bytes 786440 | tf_op jit(solution)/shard_map/ppermute | solution.py:400
  25.8 1.6 %collective-permute-start.6 = (bf16[512,256]{1,0:T(8,128)(2,1)S(1)}, bf16[512,256]{1,0:T(8,128)(2,1)S(1)}, u32[]{:S(2)}, u32[]{:S(2)}) collective-permute-start(bf16[512,256]{1,0:T(8,128)(2,1)S(1)} %pad_maximum_fusion.1.rest_0_), channel_id=1, source_target_pairs={{0,64},{16,80},{32,96},{48,112},{64,0},{80,16},{96,32},{112,48},{1... | collective-permute-start | bytes 786440 | tf_op jit(solution)/shard_map/ppermute | solution.py:400
  27.4 0.0 copy-done.6
  27.4 0.0 copy-done.7
  27.4 0.1 collective-permute-start.3
  27.5 0.0 copy-done.2
  27.6 0.6 collective-permute-start.1
  28.1 0.0 copy-done.3
  28.2 0.5 collective-permute-done.3
  28.7 0.2 collective-permute-start.2
  28.8 7.6 %collective-permute-done.8.rest_3_ = bf16[512,256]{1,0:T(8,128)(2,1)S(1)} collective-permute-done((bf16[512,256]{1,0:T(8,128)(2,1)S(1)}, bf16[512,256]{1,0:T(8,128)(2,1)S(1)}, u32[]{:S(2)}, u32[]{:S(2)}) %collective-permute-start.8) | collective-permute-done | bytes 262176 | tf_op jit(solution)/shard_map/ppermute | solution.py:400
  36.5 0.0 collective-permute-done.7.rest_2_
  36.5 1.8 %collective-permute-done.6.rest_1_ = bf16[512,256]{1,0:T(8,128)(2,1)S(1)} collective-permute-done((bf16[512,256]{1,0:T(8,128)(2,1)S(1)}, bf16[512,256]{1,0:T(8,128)(2,1)S(1)}, u32[]{:S(2)}, u32[]{:S(2)}) %collective-permute-start.6) | collective-permute-done | bytes 262176 | tf_op jit(solution)/shard_map/ppermute | solution.py:400
  38.3 0.0 collective-permute-done.1
  38.3 0.0 collective-permute-done.2
  38.3 0.0 copy-done.1
  38.3 10.2 %attention.1 = (bf16[2,512,128]{2,1,0:T(8,128)(2,1)S(1)}, bf16[2,512,128]{2,1,0:T(8,128)(2,1)S(1)}, f32[512,256]{1,0:T(8,128)S(1)}, bf16[512,256]{1,0:T(8,128)(2...) custom-call(s32[32]{0:T(128)S(1)} %copy-done.1, bf16[2,512,128]{2,1,0:T(8,128)(2,1)S(1)} %bitcast.27, ...), custom_call_target="tpu_custom_call" | custom-call | flops 3221225472 | bytes 6291456 | tf_op jit(solution)/shard_map/attention/pallas_call | solution.py:167
  48.5 3.5 %collective-permute-start.11 = (bf16[512,256]{1,0:T(8,128)(2,1)S(1)}, bf16[512,256]{1,0:T(8,128)(2,1)S(1)}, u32[]{:S(2)}, u32[]{:S(2)}) collective-permute-start(bf16[512,256]{1,0:T(8,128)(2,1)S(1)} %get-tuple-element.37), channel_id=1, source_target_pairs={{0,128},{16,144},{32,160},{48,176},{64,192},{80,208},{96,224},{112... | collective-permute-start | bytes 786440 | tf_op jit(solution)/shard_map/ppermute | solution.py:400
  52.0 0.0 collective-permute-start.12
  52.0 1.3 %collective-permute-start.10 = (bf16[512,256]{1,0:T(8,128)(2,1)S(1)}, bf16[512,256]{1,0:T(8,128)(2,1)S(1)}, u32[]{:S(2)}, u32[]{:S(2)}) collective-permute-start(bf16[512,256]{1,0:T(8,128)(2,1)S(1)} %get-tuple-element.32), channel_id=1, source_target_pairs={{0,64},{16,80},{32,96},{48,112},{64,0},{80,16},{96,32},{112,48},{1... | collective-permute-start | bytes 786440 | tf_op jit(solution)/shard_map/ppermute | solution.py:400
  53.3 0.0 all-to-all-done.in_ref
  53.3 10.6 %experts.1 = bf16[16,160,128]{2,1,0:T(8,128)(2,1)} custom-call(bf16[16,320,128]{2,1,0:T(8,128)(2,1)} %all-to-all-done.in_ref, bf16[1,2048,768]{2,1,0:T(8,128)(2,1)} %rest_0_.1, bf16[1,2048,768]{2,1,0:T(8,128)(2,1)} %rest_1_.1, bf16[1,768,2048]{2,1,0:T(8,128)(2,1)} %rest_2_.1), custom_call_target="tpu_custom_call" | custom-call | flops 2516582400 | bytes 11534336 | tf_op jit(solution)/shard_map/experts/pallas_call | solution.py:316
  63.9 7.5 %all-to-all-start.1 = ((bf16[16,160,128]{2,1,0:T(8,128)(2,1)}), bf16[16,160,128]{2,1,0:T(8,128)(2,1)S(1)}, u32[]{:S(2)}, u32[]{:S(2)}) async-start(bf16[16,160,128]{2,1,0:T(8,128)(2,1)} %experts.1), calls=%async_computation.1 | async-start | bytes 1310720 | tf_op jit(solution)/shard_map/all_to_all | solution.py:442
  71.4 0.0 copy-start
  71.4 0.0 collective-permute-done.11
  71.4 0.0 collective-permute-done.12
  71.4 0.0 collective-permute-done.10
  71.4 0.1 convert_add_fusion
  71.6 0.3 collective-permute-start.13
  71.9 0.8 collective-permute-start.15
  72.7 2.6 %collective-permute-start.14 = (bf16[128,256]{1,0:T(8,128)(2,1)S(1)}, bf16[128,256]{1,0:T(8,128)(2,1)S(1)}, u32[]{:S(2)}, u32[]{:S(2)}) collective-permute-start(bf16[128,256]{1,0:T(8,128)(2,1)S(1)} %get-tuple-element.50), channel_id=1, source_target_pairs={{0,16},{16,0},{32,48},{48,32},{64,80},{80,64},{96,112},{112,96},{1... | collective-permute-start | bytes 196616 | tf_op jit(solution)/shard_map/ppermute | solution.py:400
  75.3 0.0 collective-permute-start.9
  75.3 3.2 %collective-permute-done.13 = bf16[128,256]{1,0:T(8,128)(2,1)S(1)} collective-permute-done((bf16[128,256]{1,0:T(8,128)(2,1)S(1)}, bf16[128,256]{1,0:T(8,128)(2,1)S(1)}, u32[]{:S(2)}, u32[]{:S(2)}) %collective-permute-start.13) | collective-permute-done | bytes 65568 | tf_op jit(solution)/shard_map/ppermute | solution.py:400
  78.5 0.0 collective-permute-done.15
  78.5 0.0 collective-permute-done.14
  78.6 0.7 copy.22
  79.3 0.7 copy.21
  80.0 0.0 collective-permute-done.9
  80.1 0.9 pad_maximum_fusion
  80.9 9.2 %all-to-all-done.1.back_ref = bf16[16,160,128]{2,1,0:T(8,128)(2,1)S(1)} async-done(((bf16[16,160,128]{2,1,0:T(8,128)(2,1)}), bf16[16,160,128]{2,1,0:T(8,128)(2,1)S(1)}, u32[]{:S(2)}, u32[]{:S(2)}) %all-to-all-start.1) | async-done | bytes 655392 | tf_op jit(solution)/shard_map/all_to_all | solution.py:442
  90.1 0.0 copy-done
  90.1 1.5 %combine.1 = bf16[128,2048]{1,0:T(8,128)(2,1)} custom-call(f32[160,128]{1,0:T(8,128)S(1)} %copy-done, bf16[16,160,128]{2,1,0:T(8,128)(2,1)S(1)} %all-to-all-done.1.back_ref), custom_call_target="tpu_custom_call" | custom-call | tf_op jit(solution)/shard_map/combine/pallas_call | solution.py:362
  (15 shorter events, 0.4 us)
Async XLA Ops:
  0.6 13.6 %copy-start.5 = (bf16[128,2,128]{2,1,0:T(2,128)(2,1)S(1)}, bf16[128,2,128]{2,1,0:T(2,128)(2,1)}, u32[]{:S(2)}) copy-start(bf16[128,2,128]{2,1,0:T(2,128)(2,1)} %param.17) | copy-start | bytes 196612
  0.6 13.6 %copy-start.4 = (bf16[128,2,128]{2,1,0:T(2,128)(2,1)S(1)}, bf16[128,2,128]{2,1,0:T(2,128)(2,1)}, u32[]{:S(2)}) copy-start(bf16[128,2,128]{2,1,0:T(2,128)(2,1)} %param.16) | copy-start | bytes 196612
  0.7 26.7 %copy-start.6 = (f32[128,16]{0,1:T(8,128)S(1)}, f32[128,16]{0,1:T(8,128)}, u32[]{:S(2)}) copy-start(f32[128,16]{0,1:T(8,128)} %param.20) | copy-start | bytes 24580
  0.7 26.7 %copy-start.7 = (f32[128,16]{0,1:T(8,128)S(1)}, f32[128,16]{0,1:T(8,128)}, u32[]{:S(2)}) copy-start(f32[128,16]{0,1:T(8,128)} %param.19) | copy-start | bytes 24580
  0.7 26.8 %copy-start.2 = (bf16[128,16,128]{2,1,0:T(8,128)(2,1)S(1)}, bf16[128,16,128]{2,1,0:T(8,128)(2,1)}, u32[]{:S(2)}) copy-start(bf16[128,16,128]{2,1,0:T(8,128)(2,1)} %param.15) | copy-start | bytes 1572868
  0.7 27.4 %copy-start.3 = (bf16[128,16,128]{2,1,0:T(8,128)(2,1)S(1)}, bf16[128,16,128]{2,1,0:T(8,128)(2,1)}, u32[]{:S(2)}) copy-start(bf16[128,16,128]{2,1,0:T(8,128)(2,1)} %param.18) | copy-start | bytes 1572868
  4.7 33.6 %copy-start.1 = (s32[32]{0:T(128)S(1)}, s32[32]{0:T(128)}, u32[]{:S(2)}) copy-start(s32[32]{0:T(128)} %span_ref.1) | copy-start | bytes 388
  4.7 48.6 %all-to-all-start = ((bf16[16,320,128]{2,1,0:T(8,128)(2,1)}), bf16[16,320,128]{2,1,0:T(8,128)(2,1)}, u32[]{:S(2)}, u32[]{:S(2)}) async-start(bf16[16,320,128]{2,1,0:T(8,128)(2,1)} %get-tuple-element.31), calls=%async_computation | async-start | bytes 2621440 | tf_op jit(solution)/shard_map/all_to_all | solution.py:411
  14.3 3.0 %collective-permute-start.4 = (bf16[128,256]{1,0:T(8,128)(2,1)S(1)}, bf16[128,256]{1,0:T(8,128)(2,1)S(1)}, u32[]{:S(2)}, u32[]{:S(2)}) collective-permute-start(bf16[128,256]{1,0:T(8,128)(2,1)S(1)} %select_bitcast_fusion.2), channel_id=1, source_target_pairs={{0,16},{16,0},{32,48},{48,32},{64,80},{80,64},{96,112},{112,96},{1... | collective-permute-start | bytes 196616 | tf_op jit(solution)/shard_map/ppermute | solution.py:400
  14.4 5.9 %collective-permute-start.5 = (bf16[128,256]{1,0:T(8,128)(2,1)S(1)}, bf16[128,256]{1,0:T(8,128)(2,1)S(1)}, u32[]{:S(2)}, u32[]{:S(2)}) collective-permute-start(bf16[128,256]{1,0:T(8,128)(2,1)S(1)} %select_bitcast_fusion.2), channel_id=1, source_target_pairs={{0,48},{16,32},{32,16},{48,0},{64,112},{80,96},{96,80},{112,64},{1... | collective-permute-start | bytes 196616 | tf_op jit(solution)/shard_map/ppermute | solution.py:400
  17.3 5.9 %collective-permute-start = (bf16[128,256]{1,0:T(8,128)(2,1)S(1)}, bf16[128,256]{1,0:T(8,128)(2,1)S(1)}, u32[]{:S(2)}, u32[]{:S(2)}) collective-permute-start(bf16[128,256]{1,0:T(8,128)(2,1)S(1)} %get-tuple-element.47), channel_id=1, source_target_pairs={{0,32},{16,48},{32,0},{48,16},{64,96},{80,112},{96,64},{112,80},{1... | collective-permute-start | bytes 196616 | tf_op jit(solution)/shard_map/ppermute | solution.py:400
  23.2 13.2 %collective-permute-start.8 = (bf16[512,256]{1,0:T(8,128)(2,1)S(1)}, bf16[512,256]{1,0:T(8,128)(2,1)S(1)}, u32[]{:S(2)}, u32[]{:S(2)}) collective-permute-start(bf16[512,256]{1,0:T(8,128)(2,1)S(1)} %pad_maximum_fusion.1.rest_0_), channel_id=1, source_target_pairs={{0,192},{16,208},{32,224},{48,240},{64,128},{80,144},{96,160},{112... | collective-permute-start | bytes 786440 | tf_op jit(solution)/shard_map/ppermute | solution.py:400
  24.9 11.6 %collective-permute-start.7 = (bf16[512,256]{1,0:T(8,128)(2,1)S(1)}, bf16[512,256]{1,0:T(8,128)(2,1)S(1)}, u32[]{:S(2)}, u32[]{:S(2)}) collective-permute-start(bf16[512,256]{1,0:T(8,128)(2,1)S(1)} %pad_maximum_fusion.1.rest_0_), channel_id=1, source_target_pairs={{0,128},{16,144},{32,160},{48,176},{64,192},{80,208},{96,224},{112... | collective-permute-start | bytes 786440 | tf_op jit(solution)/shard_map/ppermute | solution.py:400
  25.8 12.5 %collective-permute-start.6 = (bf16[512,256]{1,0:T(8,128)(2,1)S(1)}, bf16[512,256]{1,0:T(8,128)(2,1)S(1)}, u32[]{:S(2)}, u32[]{:S(2)}) collective-permute-start(bf16[512,256]{1,0:T(8,128)(2,1)S(1)} %pad_maximum_fusion.1.rest_0_), channel_id=1, source_target_pairs={{0,64},{16,80},{32,96},{48,112},{64,0},{80,16},{96,32},{112,48},{1... | collective-permute-start | bytes 786440 | tf_op jit(solution)/shard_map/ppermute | solution.py:400
  27.4 1.3 %collective-permute-start.3 = (f32[2,8,128]{2,1,0:T(8,128)S(1)}, f32[2,8,128]{2,1,0:T(8,128)S(1)}, u32[]{:S(2)}, u32[]{:S(2)}) collective-permute-start(f32[2,8,128]{2,1,0:T(8,128)S(1)} %get-tuple-element.61), channel_id=1, source_target_pairs={{0,16},{16,0},{32,48},{48,32},{64,80},{80,64},{96,112},{112,96},{1... | collective-permute-start | bytes 24584 | tf_op jit(solution)/shard_map/ppermute | solution.py:400
  27.6 10.7 %collective-permute-start.1 = (bf16[128,8,128]{2,1,0:T(8,128)(2,1)S(1)}, bf16[128,8,128]{2,1,0:T(8,128)(2,1)S(1)}, u32[]{:S(2)}, u32[]{:S(2)}) collective-permute-start(bf16[128,8,128]{2,1,0:T(8,128)(2,1)S(1)} %get-tuple-element.55), channel_id=1, source_target_pairs={{0,16},{16,0},{32,48},{48,32},{64,80},{80,64},{96,112},{112,96},{1... | collective-permute-start | bytes 786440 | tf_op jit(solution)/shard_map/ppermute | solution.py:400
  28.7 9.6 %collective-permute-start.2 = (bf16[128,8,128]{2,1,0:T(8,128)(2,1)S(1)}, bf16[128,8,128]{2,1,0:T(8,128)(2,1)S(1)}, u32[]{:S(2)}, u32[]{:S(2)}) collective-permute-start(bf16[128,8,128]{2,1,0:T(8,128)(2,1)S(1)} %get-tuple-element.53), channel_id=1, source_target_pairs={{0,16},{16,0},{32,48},{48,32},{64,80},{80,64},{96,112},{112,96},{1... | collective-permute-start | bytes 786440 | tf_op jit(solution)/shard_map/ppermute | solution.py:400
  48.5 22.9 %collective-permute-start.11 = (bf16[512,256]{1,0:T(8,128)(2,1)S(1)}, bf16[512,256]{1,0:T(8,128)(2,1)S(1)}, u32[]{:S(2)}, u32[]{:S(2)}) collective-permute-start(bf16[512,256]{1,0:T(8,128)(2,1)S(1)} %get-tuple-element.37), channel_id=1, source_target_pairs={{0,128},{16,144},{32,160},{48,176},{64,192},{80,208},{96,224},{112... | collective-permute-start | bytes 786440 | tf_op jit(solution)/shard_map/ppermute | solution.py:400
  52.0 19.4 %collective-permute-start.12 = (bf16[512,256]{1,0:T(8,128)(2,1)S(1)}, bf16[512,256]{1,0:T(8,128)(2,1)S(1)}, u32[]{:S(2)}, u32[]{:S(2)}) collective-permute-start(bf16[512,256]{1,0:T(8,128)(2,1)S(1)} %get-tuple-element.38), channel_id=1, source_target_pairs={{0,192},{16,208},{32,224},{48,240},{64,128},{80,144},{96,160},{112... | collective-permute-start | bytes 786440 | tf_op jit(solution)/shard_map/ppermute | solution.py:400
  52.0 19.4 %collective-permute-start.10 = (bf16[512,256]{1,0:T(8,128)(2,1)S(1)}, bf16[512,256]{1,0:T(8,128)(2,1)S(1)}, u32[]{:S(2)}, u32[]{:S(2)}) collective-permute-start(bf16[512,256]{1,0:T(8,128)(2,1)S(1)} %get-tuple-element.32), channel_id=1, source_target_pairs={{0,64},{16,80},{32,96},{48,112},{64,0},{80,16},{96,32},{112,48},{1... | collective-permute-start | bytes 786440 | tf_op jit(solution)/shard_map/ppermute | solution.py:400
  63.9 26.2 %all-to-all-start.1 = ((bf16[16,160,128]{2,1,0:T(8,128)(2,1)}), bf16[16,160,128]{2,1,0:T(8,128)(2,1)S(1)}, u32[]{:S(2)}, u32[]{:S(2)}) async-start(bf16[16,160,128]{2,1,0:T(8,128)(2,1)} %experts.1), calls=%async_computation.1 | async-start | bytes 1310720 | tf_op jit(solution)/shard_map/all_to_all | solution.py:442
  71.4 18.8 %copy-start = (f32[160,128]{1,0:T(8,128)S(1)}, f32[160,128]{1,0:T(8,128)}, u32[]{:S(2)}) copy-start(f32[160,128]{1,0:T(8,128)} %get-tuple-element.39.weight_ref) | copy-start | bytes 245764
  71.6 6.9 %collective-permute-start.13 = (bf16[128,256]{1,0:T(8,128)(2,1)S(1)}, bf16[128,256]{1,0:T(8,128)(2,1)S(1)}, u32[]{:S(2)}, u32[]{:S(2)}) collective-permute-start(bf16[128,256]{1,0:T(8,128)(2,1)S(1)} %get-tuple-element.48), channel_id=1, source_target_pairs={{0,32},{16,48},{32,0},{48,16},{64,96},{80,112},{96,64},{112,80},{1... | collective-permute-start | bytes 196616 | tf_op jit(solution)/shard_map/ppermute | solution.py:400
  71.9 6.6 %collective-permute-start.15 = (bf16[128,256]{1,0:T(8,128)(2,1)S(1)}, bf16[128,256]{1,0:T(8,128)(2,1)S(1)}, u32[]{:S(2)}, u32[]{:S(2)}) collective-permute-start(bf16[128,256]{1,0:T(8,128)(2,1)S(1)} %get-tuple-element.49), channel_id=1, source_target_pairs={{0,48},{16,32},{32,16},{48,0},{64,112},{80,96},{96,80},{112,64},{1... | collective-permute-start | bytes 196616 | tf_op jit(solution)/shard_map/ppermute | solution.py:400
  72.7 5.8 %collective-permute-start.14 = (bf16[128,256]{1,0:T(8,128)(2,1)S(1)}, bf16[128,256]{1,0:T(8,128)(2,1)S(1)}, u32[]{:S(2)}, u32[]{:S(2)}) collective-permute-start(bf16[128,256]{1,0:T(8,128)(2,1)S(1)} %get-tuple-element.50), channel_id=1, source_target_pairs={{0,16},{16,0},{32,48},{48,32},{64,80},{80,64},{96,112},{112,96},{1... | collective-permute-start | bytes 196616 | tf_op jit(solution)/shard_map/ppermute | solution.py:400
  75.3 4.7 %collective-permute-start.9 = (bf16[2,512,128]{2,1,0:T(8,128)(2,1)S(1)}, bf16[2,512,128]{2,1,0:T(8,128)(2,1)S(1)}, u32[]{:S(2)}, u32[]{:S(2)}) collective-permute-start(bf16[2,512,128]{2,1,0:T(8,128)(2,1)S(1)} %get-tuple-element.34), channel_id=1, source_target_pairs={{0,16},{16,0},{32,48},{48,32},{64,80},{80,64},{96,112},{112,96},{1... | collective-permute-start | bytes 786440 | tf_op jit(solution)/shard_map/ppermute | solution.py:400
where the time goes:
time: 91.7 us
  starting transfers between devices  34.7 us (38%)
  waiting for transfers between devices  27 us (29%)
  Pallas kernels  26.3 us (29%)
  local copies, waits for them, and re-layouts  1.47 us (2%)
  other arithmetic  1.31 us (1%)
  between operations  0.93 us (1%)
    ppermute x16, waiting for transfers between devices, on_device(): lax.ppermute(array, 'ctx', [(i, i ^ k) for i in range(members)])  17.8 us
    ppermute x16, starting transfers between devices, on_device(): lax.ppermute(array, 'ctx', [(i, i ^ k) for i in range(members)])  17.7 us
    pallas_call x1, Pallas kernels, mlp(): pl.pallas_call(mlp_kernel, out_shape=jax.ShapeDtypeStruct((sources, block...  10.6 us
    pallas_call x1, Pallas kernels, attention(): pl.pallas_call(functools.partial(attention_kernel, scale, blocks), out_sh...  10.2 us
    all_to_all x1, starting transfers between devices, on_device(): lax.all_to_all(send, 'exp', split_axis=0, concat_axis=0, tiled=True)  9.55 us
    all_to_all x1, waiting for transfers between devices, on_device(): lax.all_to_all(slot_grad, 'exp', split_axis=0, concat_axis=0, tiled=True)  9.19 us
    all_to_all x1, starting transfers between devices, on_device(): lax.all_to_all(slot_grad, 'exp', split_axis=0, concat_axis=0, tiled=True)  7.47 us
    pallas_call x1, Pallas kernels, dispatch(): pl.pallas_call(dispatch_kernel, out_shape=(jax.ShapeDtypeStruct((experts,...  3.96 us
  transfers between devices with their start and end apart: 18, of which 7 were waited for; matrix products, arithmetic and copies ran while one was open for 3% of the time, Pallas kernels for 23%

commit v1 on v0

--- a/solution.py
+++ b/solution.py
@@ -39,33 +39,36 @@
     return high, middle, (rest - middle.astype(F32)).astype(BF16)
 
 
-def attention_kernel(
-    scale,
-    kv_blocks,
-    span_ref,
-    q_own,
-    q_got,
-    d_own,
-    d_got,
-    stat_own,
-    stat_got,
-    *rest,
+def span_finder(span_ref):
+    slots = span_ref.shape[0]
+
+    def span_of(chip, core, upper):
+        place = chip * 2 + core
+        return span_ref[slots - 1 - place if upper else place]
+
+    return span_of
+
+
+def pair_gradients(scale, queries, grads, norm, inner, keys, values, keys_t, visible):
+    scores = dot_rows(keys, queries)
+    probs = jnp.exp2(scores * (scale / math.log(2.0)) - norm)
+    if visible is not None:
+        probs = jnp.where(visible(scores.shape), probs, 0.0)
+    dprobs = dot_rows(values, grads)
+    dscores = (probs * (dprobs - inner)).astype(BF16)
+    return dot(dscores, queries), dot(probs.astype(BF16), grads), dot(keys_t, dscores)
+
+
+def near_kernel(
+    scale, span_ref, q_own, q_got, d_own, d_got, stat_own, stat_got, kv_ref, dq_ref, sum_ref, stat_ref, keys_t, key_pos
 ):
-    kv_refs = rest[:kv_blocks]
-    dq_own, dq_got, own_ref = rest[kv_blocks : kv_blocks + 3]
-    part_refs = rest[kv_blocks + 3 : 2 * kv_blocks + 2]
-    keys, values, keys_t, dk_acc, dv_acc, dq_acc, stat_acc = rest[2 * kv_blocks + 2 :]
     me = lax.axis_index("ctx")
-    chip = me // 2
-    core = me % 2
-    slots = span_ref.shape[0]
-    half = keys.shape[0] // slots
+    chip, core = me // 2, me % 2
+    span_of = span_finder(span_ref)
     width = q_own.shape[1]
+    count = kv_ref.shape[0]
+    half = count // 8
     repeat = width // half
-
-    def span_of(chip_index, core_index, upper):
-        place = chip_index * 2 + core_index
-        return span_ref[slots - 1 - place if upper else place]
 
     stats = jnp.concatenate([stat_own[...], stat_got[...]], axis=0)
     rows = stats.shape[1]
@@ -76,102 +79,174 @@
     ).astype(F32).astype(BF16)
     high, middle, low = split3(stats)
     lanes = dot(high, spread) + (dot(middle, spread) + dot(low, spread))
-    count = stats.shape[0] // repeat
-    lanes = lanes.reshape(count, repeat, wide)
+    lanes = lanes.reshape(stats.shape[0] // repeat, repeat, wide)
     head = lax.broadcasted_iota(jnp.int32, lanes.shape, 1)
     lane_head = lax.broadcasted_iota(jnp.int32, lanes.shape, 2) % repeat
-    stat_acc[...] = jnp.sum(jnp.where(head == lane_head, lanes, 0.0), axis=1)
+    lanes = jnp.sum(jnp.where(head == lane_head, lanes, 0.0), axis=1)
+    is_norm = lax.broadcasted_iota(jnp.int32, lanes.shape, 0) % 2 == 0
+    stat_ref[...] = jnp.where(is_norm, lanes * (1.0 / math.log(2.0)), lanes)
+
+    keys_t[...] = kv_ref[:, :LANES].T
+    for part in range(8):
+        span = span_of(chip ^ (part // 4), part // 2 % 2, part % 2)
+        at = slice(part * half, (part + 1) * half)
+        key_pos[at, :] = span * half + lax.broadcasted_iota(jnp.int32, (half, LANES), 0)
+
+    for index in range(4):
+        upper = index % 2
+        q_ref, d_ref, who = (q_own, d_own, core) if index < 2 else (q_got, d_got, 1 - core)
+        line = 2 * (index // 2)
+        span = span_of(chip, who, upper)
+
+        def visible(shape):
+            query_pos = span * half + lax.broadcasted_iota(jnp.int32, shape, 1) // repeat
+            return jnp.concatenate([key_pos[...]] * (width // LANES), axis=1) <= query_pos
+
+        at = slice(upper * width, (upper + 1) * width)
+        dk, dv, dq = pair_gradients(
+            scale,
+            q_ref[upper],
+            d_ref[upper],
+            stat_ref[line : line + 1, at],
+            stat_ref[line + 1 : line + 2, at],
+            kv_ref[:, :LANES],
+            kv_ref[:, LANES:],
+            keys_t[...],
+            visible,
+        )
+        dq_ref[index] = dq
+        dk = dk * scale
+        sum_ref[:, :LANES] = dk if index == 0 else sum_ref[:, :LANES] + dk
+        sum_ref[:, LANES:] = dv if index == 0 else sum_ref[:, LANES:] + dv
+
+
+def far_kernel(scale, kv_blocks, span_ref, q_own, q_got, d_own, d_got, stat_ref, dq_ref, *rest):
+    kv_refs = rest[:kv_blocks]
+    dq_own, dq_got = rest[kv_blocks : kv_blocks + 2]
+    part_refs = rest[kv_blocks + 2 : 2 * kv_blocks + 2]
+    keys, values, keys_t, dk_acc, dv_acc, dq_acc, before = rest[2 * kv_blocks + 2 :]
+    me = lax.axis_index("ctx")
+    chip, core = me // 2, me % 2
+    span_of = span_finder(span_ref)
+    slots = span_ref.shape[0]
+    width = q_own.shape[1]
+    half = kv_refs[0].shape[0] // 8
+
+    for n in range(slots):
+        before[n] = 0
+    spans = [
+        [span_of(chip ^ (2 * (block + 1) + part // 4), part // 2 % 2, part % 2) for part in range(8)]
+        for block in range(kv_blocks)
+    ]
+    for line in spans:
+        for span in line:
+            before[span] = 1
+    running = 0
+    for n in range(slots):
+        here = before[n]
+        before[n] = running
+        running = running + here
+
+    def place(block, part):
+        return pl.ds(pl.multiple_of(before[spans[block][part]] * half, half), half)
 
     for block in range(kv_blocks):
         for part in range(8):
-            span = span_of(chip ^ (2 * block + part // 4), part // 2 % 2, part % 2)
-            at = pl.ds(pl.multiple_of(span * half, half), half)
+            at = place(block, part)
             rows = kv_refs[block][part * half : (part + 1) * half, :]
             keys[at, :] = rows[:, :LANES]
             values[at, :] = rows[:, LANES:]
-    chunks = keys.shape[0] // CHUNK
-    for chunk in range(chunks):
+    for chunk in range(keys.shape[0] // CHUNK):
         at = slice(chunk * CHUNK, (chunk + 1) * CHUNK)
         keys_t[:, at] = keys[at, :].T
     dk_acc[...] = jnp.zeros_like(dk_acc)
     dv_acc[...] = jnp.zeros_like(dv_acc)
-    factor = scale / math.log(2.0)
 
     for index in range(4):
         upper = index % 2
-        if index < 2:
-            q_ref, d_ref, dq_ref, who = q_own, d_own, dq_own, core
-        else:
-            q_ref, d_ref, dq_ref, who = q_got, d_got, dq_got, 1 - core
+        q_ref, d_ref, out_ref, who = (q_own, d_own, dq_own, core) if index < 2 else (q_got, d_got, dq_got, 1 - core)
         line = 2 * (index // 2)
-        span = span_of(chip, who, upper)
+        lanes = slice(upper * width, (upper + 1) * width)
         queries = q_ref[upper]
         grads = d_ref[upper]
-        norm = stat_acc[line : line + 1, upper * width : (upper + 1) * width] * (1.0 / math.log(2.0))
-        inner = stat_acc[line + 1 : line + 2, upper * width : (upper + 1) * width]
-        dq_acc[...] = jnp.zeros_like(dq_acc)
+        norm = stat_ref[line : line + 1, lanes]
+        inner = stat_ref[line + 1 : line + 2, lanes]
+        dq_acc[...] = dq_ref[index]
+        ahead = before[span_of(chip, who, upper)] * half
 
         def one(start, count, masked):
             at = pl.ds(pl.multiple_of(start, CHUNK), count)
-            scores = dot_rows(keys[at, :], queries)
-            probs = jnp.exp2(scores * factor - norm)
-            if masked:
-                key_pos = start + lax.broadcasted_iota(jnp.int32, scores.shape, 0)
-                query_pos = span * half + lax.broadcasted_iota(jnp.int32, scores.shape, 1) // repeat
-                probs = jnp.where(key_pos <= query_pos, probs, 0.0)
-            dprobs = dot_rows(values[at, :], grads)
-            dscores = (probs * (dprobs - inner)).astype(BF16)
-            dv_acc[at, :] += dot(probs.astype(BF16), grads)
-            dk_acc[at, :] += dot(dscores, queries)
-            dq_acc[...] += dot(keys_t[:, at], dscores)
-
-        ahead = span * half
-        lax.fori_loop(0, ahead // LONG, lambda i, none: (one(i * LONG, LONG, False), none)[1], 0)
-        rest_start = ahead // LONG * LONG
-
-        @pl.when(ahead - rest_start >= LONG // 2)
+            seen = lambda shape: start + lax.broadcasted_iota(jnp.int32, shape, 0) < ahead
+            dk, dv, dq = pair_gradients(
+                scale, queries, grads, norm, inner, keys[at, :], values[at, :], keys_t[:, at], seen if masked else None
+            )
+            dk_acc[at, :] += dk
+            dv_acc[at, :] += dv
+            dq_acc[...] += dq
+
+        long = ahead // LONG * LONG
+        tail = ahead // (LONG // 2) * (LONG // 2)
+
+        @pl.when(long > 0)
         def _():
-            one(rest_start, LONG // 2, False)
-
-        tail = ahead // (LONG // 2) * (LONG // 2)
-
-        @pl.when(ahead - tail >= CHUNK)
+            one(0, LONG, False)
+
+        @pl.when(tail > long)
+        def _():
+            one(long, LONG // 2, False)
+
+        @pl.when(ahead - tail > CHUNK)
         def _():
             one(tail, LONG // 2, True)
 
-        @pl.when(ahead - tail < CHUNK)
+        @pl.when((ahead > tail) & (ahead - tail <= CHUNK))
         def _():
             one(tail, CHUNK, True)
 
-        dq_ref[upper] = (dq_acc[...].T * scale).astype(BF16)
+        out_ref[upper] = (dq_acc[...].T * scale).astype(BF16)
 
     for block in range(kv_blocks):
         for part in range(8):
-            span = span_of(chip ^ (2 * block + part // 4), part // 2 % 2, part % 2)
-            at = pl.ds(pl.multiple_of(span * half, half), half)
+            at = place(block, part)
             rows = slice(part * half, (part + 1) * half)
-            if block == 0:
-                own_ref[rows, :LANES] = dk_acc[at, :] * scale
-                own_ref[rows, LANES:] = dv_acc[at, :]
-            else:
-                part_refs[block - 1][rows, :LANES] = (dk_acc[at, :] * scale).astype(BF16)
-                part_refs[block - 1][rows, LANES:] = dv_acc[at, :].astype(BF16)
-
-
-def attention(span_order, q_own, q_got, d_own, d_got, stat_own, stat_got, kv_list, scale):
+            part_refs[block][rows, :LANES] = (dk_acc[at, :] * scale).astype(BF16)
+            part_refs[block][rows, LANES:] = dv_acc[at, :].astype(BF16)
+
+
+def attention_near(span_order, q_own, q_got, d_own, d_got, stat_own, stat_got, kv, scale):
+    count = kv.shape[0]
+    halves, width, size = q_own.shape
+    assert count * 2 == LONG
+    return pl.pallas_call(
+        functools.partial(near_kernel, scale),
+        out_shape=(
+            jax.ShapeDtypeStruct((2 * halves, size, width), F32),
+            jax.ShapeDtypeStruct((count, 2 * LANES), F32),
+            jax.ShapeDtypeStruct((4, halves * width), F32),
+        ),
+        in_specs=[SMEM] + [VMEM] * 7,
+        out_specs=(VMEM,) * 3,
+        scratch_shapes=[pltpu.VMEM((LANES, count), BF16), pltpu.VMEM((count, LANES), jnp.int32)],
+        compiler_params=pltpu.CompilerParams(vmem_limit_bytes=16 * MIB),
+        cost_estimate=pl.CostEstimate(
+            flops=20 * halves * width * count * size,
+            bytes_accessed=3 * MIB,
+            transcendentals=2 * halves * width * count,
+        ),
+        name="attention_near",
+    )(span_order, q_own, q_got, d_own, d_got, stat_own, stat_got, kv)
+
+
+def attention_far(span_order, q_own, q_got, d_own, d_got, stats, dq_near, kv_list, scale):
     blocks = len(kv_list)
     rows = kv_list[0].shape[0]
     total = blocks * rows
-    spans, width, _ = q_own.shape
+    halves, width, size = q_own.shape
+    assert total % LONG == LONG // 2
     part = jax.ShapeDtypeStruct((rows, 2 * LANES), BF16)
     return pl.pallas_call(
-        functools.partial(attention_kernel, scale, blocks),
-        out_shape=(
-            jax.ShapeDtypeStruct(q_own.shape, BF16),
-            jax.ShapeDtypeStruct(q_own.shape, BF16),
-            jax.ShapeDtypeStruct((rows, 2 * LANES), F32),
-        )
-        + (part,) * (blocks - 1),
+        functools.partial(far_kernel, scale, blocks),
+        out_shape=(jax.ShapeDtypeStruct(q_own.shape, BF16),) * 2 + (part,) * blocks,
         in_specs=[SMEM] + [VMEM] * (6 + blocks),
         out_specs=(VMEM,) * (2 + blocks),
         scratch_shapes=[
@@ -181,16 +256,16 @@
             pltpu.VMEM((total, LANES), F32),
             pltpu.VMEM((total, LANES), F32),
             pltpu.VMEM((LANES, width), F32),
-            pltpu.VMEM((4, spans * width), F32),
+            pltpu.SMEM(span_order.shape, jnp.int32),
         ],
         compiler_params=pltpu.CompilerParams(vmem_limit_bytes=16 * MIB),
         cost_estimate=pl.CostEstimate(
-            flops=6 * spans * width * total * LANES * 2,
-            bytes_accessed=6 * 1024 * 1024,
-            transcendentals=spans * width * total // 12,
+            flops=20 * halves * width * total * size,
+            bytes_accessed=6 * MIB,
+            transcendentals=2 * halves * width * total,
         ),
-        name="attention",
-    )(span_order, q_own, q_got, d_own, d_got, stat_own, stat_got, *kv_list)
+        name="attention_far",
+    )(span_order, q_own, q_got, d_own, d_got, stats, dq_near, *kv_list)
 
 
 def slots_to_chunks(tiles, experts, blocks, chunk_ref, first):
@@ -409,7 +484,7 @@
     ordered = lambda mine, other: [jnp.where(first, mine, other), jnp.where(first, other, mine)]
     kv_pair = jnp.concatenate(ordered(kv_own, kv_got) + ordered(kv_near, kv_cross), axis=0)
     received = lax.all_to_all(send, "exp", split_axis=0, concat_axis=0, tiled=True)
-    kv_list = [kv_pair] + [trade(kv_pair, 4 * k) for k in range(1, chips // 2)]
+    kv_list = [trade(kv_pair, 4 * k) for k in range(1, chips // 2)]
 
     kv_near, queries, out_grad, log_norm, out_dot = lax.optimization_barrier(
         (kv_near, queries, out_grad, log_norm, out_dot)
@@ -426,17 +501,11 @@
     stat_got = trade(stat_away, 1)
 
     spans = lambda array: array.reshape(2, rows // 2 * group, size)
-    dq_own, dq_got, own_sum, *parts = attention(
-        span_order,
-        spans(q_own),
-        spans(q_got),
-        spans(d_own),
-        spans(d_got),
-        stat_own.reshape(2 * group, rows),
-        stat_got.reshape(2 * group, rows),
-        kv_list,
-        scale,
+    shared = (span_order, spans(q_own), spans(q_got), spans(d_own), spans(d_got))
+    dq_near, own_sum, stats = attention_near(
+        *shared, stat_own.reshape(2 * group, rows), stat_got.reshape(2 * group, rows), kv_pair, scale
     )
+    dq_own, dq_got, *parts = attention_far(*shared, stats, dq_near, kv_list, scale)
     received, _ = lax.optimization_barrier((received, parts[0]))
     slot_grad = mlp(received, w_gate, w_up, w_down)
     returned = lax.all_to_all(slot_grad, "exp", split_axis=0, concat_axis=0, tiled=True)

time: 91.7 us -> 92.1 us (level)
  the two profiles are of different devices: /device:TPU:8 before, /device:TPU:4 now
where the time goes in v1:
time: 92.1 us; the launch traced here: 90.9 us
  starting transfers between devices  33.2 us (36%)
  Pallas kernels  28.5 us (31%)
  waiting for transfers between devices  25.5 us (28%)
  local copies, waits for them, and re-layouts  1.47 us (2%)
  other arithmetic  1.31 us (1%)
  between operations  0.94 us (1%)
    ppermute x16, waiting for transfers between devices, on_device(): lax.ppermute(array, 'ctx', [(i, i ^ k) for i in range(members)])  17 us
    ppermute x16, starting transfers between devices, on_device(): lax.ppermute(array, 'ctx', [(i, i ^ k) for i in range(members)])  15.8 us
    pallas_call x1, Pallas kernels, mlp(): pl.pallas_call(mlp_kernel, out_shape=jax.ShapeDtypeStruct((sources, block...  10.6 us
    all_to_all x1, starting transfers between devices, on_device(): lax.all_to_all(send, 'exp', split_axis=0, concat_axis=0, tiled=True)  9.26 us
    pallas_call x1, Pallas kernels, attention_far(): pl.pallas_call(functools.partial(far_kernel, scale, blocks), out_shape=(j...  9.02 us
    all_to_all x1, waiting for transfers between devices, on_device(): lax.all_to_all(slot_grad, 'exp', split_axis=0, concat_axis=0, tiled=True)  8.49 us
    all_to_all x1, starting transfers between devices, on_device(): lax.all_to_all(slot_grad, 'exp', split_axis=0, concat_axis=0, tiled=True)  8.11 us
    pallas_call x1, Pallas kernels, dispatch(): pl.pallas_call(dispatch_kernel, out_shape=(jax.ShapeDtypeStruct((experts,...  3.89 us
  transfers between devices with their start and end apart: 18, of which 7 were waited for; matrix products, arithmetic and copies ran while one was open for 3% of the time, Pallas kernels for 25%

profile of v1, /device:TPU:4, one launch (start us, length us, event | category | flops | bytes accessed | tf_op | source)
XLA Modules:
  0.0 90.9 jit_solution(5193514495557535010)
XLA Ops:
  0.6 0.0 copy-start.5
  0.6 0.0 copy-start.4
  0.7 0.0 copy-start.6
  0.7 0.0 copy-start.7
  0.7 0.0 copy-start.3
  0.7 0.0 copy-start.2
  0.7 3.9 %dispatch.1 = (bf16[16,320,128]{2,1,0:T(8,128)(2,1)}, f32[160,128]{1,0:T(8,128)}) custom-call(s32[8,128]{1,0:T(8,128)} %bitcast.40, s32[8,128]{1,0:T(8,128)} %bitcast.41, f32[8,128]{1,0:T(8,128)} %bitcast.42, bf16[128,2048]{1,0:T(8,128)(2,1)} %x_hbm.1, bf16[128,2048]{1,0:T(8,128)(2,1)} %g_hbm.1), custom_call_target="tpu_custom_call" | custom-call | tf_op jit(solution)/shard_map/dispatch/pallas_call | solution.py:322
  4.6 0.0 copy-start.1
  4.6 9.3 %all-to-all-start = ((bf16[16,320,128]{2,1,0:T(8,128)(2,1)}), bf16[16,320,128]{2,1,0:T(8,128)(2,1)}, u32[]{:S(2)}, u32[]{:S(2)}) async-start(bf16[16,320,128]{2,1,0:T(8,128)(2,1)} %get-tuple-element.35), calls=%async_computation | async-start | bytes 2621440 | tf_op jit(solution)/shard_map/all_to_all | solution.py:486
  13.9 0.0 copy-done.4
  13.9 0.0 copy-done.5
  14.0 0.1 collective-permute-start.4
  14.1 0.9 %collective-permute-start.5 = (bf16[128,256]{1,0:T(8,128)(2,1)S(1)}, bf16[128,256]{1,0:T(8,128)(2,1)S(1)}, u32[]{:S(2)}, u32[]{:S(2)}) collective-permute-start(bf16[128,256]{1,0:T(8,128)(2,1)S(1)} %select_bitcast_fusion.2), channel_id=1, source_target_pairs={{0,48},{16,32},{32,16},{48,0},{64,112},{80,96},{96,80},{112,64},{1... | collective-permute-start | bytes 196616 | tf_op jit(solution)/shard_map/ppermute | solution.py:475
  15.0 0.3 collective-permute-done.4
  15.3 2.5 %collective-permute-start = (bf16[128,256]{1,0:T(8,128)(2,1)S(1)}, bf16[128,256]{1,0:T(8,128)(2,1)S(1)}, u32[]{:S(2)}, u32[]{:S(2)}) collective-permute-start(bf16[128,256]{1,0:T(8,128)(2,1)S(1)} %get-tuple-element.51), channel_id=1, source_target_pairs={{0,32},{16,48},{32,0},{48,16},{64,96},{80,112},{96,64},{112,80},{1... | collective-permute-start | bytes 196616 | tf_op jit(solution)/shard_map/ppermute | solution.py:475
  17.8 3.6 %collective-permute-done = bf16[128,256]{1,0:T(8,128)(2,1)S(1)} collective-permute-done((bf16[128,256]{1,0:T(8,128)(2,1)S(1)}, bf16[128,256]{1,0:T(8,128)(2,1)S(1)}, u32[]{:S(2)}, u32[]{:S(2)}) %collective-permute-start) | collective-permute-done | bytes 65568 | tf_op jit(solution)/shard_map/ppermute | solution.py:475
  21.5 0.0 copy-done.6
  21.5 0.0 copy-done.7
  21.5 0.1 collective-permute-start.3
  21.6 0.0 copy-done.2
  21.6 0.6 collective-permute-start.1
  22.2 0.0 copy-done.3
  22.2 0.1 collective-permute-start.2
  22.4 0.0 collective-permute-done.5
  22.4 3.1 %collective-permute-start.8 = (bf16[512,256]{1,0:T(8,128)(2,1)S(1)}, bf16[512,256]{1,0:T(8,128)(2,1)S(1)}, u32[]{:S(2)}, u32[]{:S(2)}) collective-permute-start(bf16[512,256]{1,0:T(8,128)(2,1)S(1)} %pad_maximum_fusion.1.kv_ref), channel_id=1, source_target_pairs={{0,192},{16,208},{32,224},{48,240},{64,128},{80,144},{96,160},{112... | collective-permute-start | bytes 786440 | tf_op jit(solution)/shard_map/ppermute | solution.py:475
  25.5 0.6 collective-permute-start.7
  26.1 0.0 collective-permute-done.3
  26.1 0.5 collective-permute-start.6
  26.6 0.0 collective-permute-done.1
  26.6 0.0 collective-permute-done.2
  26.6 0.0 copy-done.1
  26.6 3.4 %attention_near.1 = (f32[4,128,512]{2,1,0:T(8,128)S(1)}, f32[512,256]{1,0:T(8,128)S(1)}, f32[4,1024]{1,0:T(4,128)S(1)}) custom-call(s32[32]{0:T(128)S(1)} %copy-done.1, bf16[2,512,128]{2,1,0:T(8,128)(2,1)S(1)} %bitcast.27, bf16[2,512,128]{2,1,0:T(8,128)(2,1)S(1)} %bitcast.31, bf16[2,512,128]{2,1,0:T(8,128)(2,1)S(1)} %bitcast.29, ...), custom_call_target="tpu_custom_call" | custom-call | flops 1342177280 | bytes 3145728 | tf_op jit(solution)/shard_map/attention_near/pallas_call | solution.py:220
  30.0 8.0 %collective-permute-done.8.rest_2_ = bf16[512,256]{1,0:T(8,128)(2,1)S(1)} collective-permute-done((bf16[512,256]{1,0:T(8,128)(2,1)S(1)}, bf16[512,256]{1,0:T(8,128)(2,1)S(1)}, u32[]{:S(2)}, u32[]{:S(2)}) %collective-permute-start.8) | collective-permute-done | bytes 262176 | tf_op jit(solution)/shard_map/ppermute | solution.py:475
  38.1 0.0 collective-permute-done.7.rest_1_
  38.1 0.7 collective-permute-done.6.rest_0_
  38.8 9.0 %attention_far.1 = (bf16[2,512,128]{2,1,0:T(8,128)(2,1)S(1)}, bf16[2,512,128]{2,1,0:T(8,128)(2,1)S(1)}, bf16[512,256]{1,0:T(8,128)(2,1)S(1)}, bf16[512,256]{1,0:T(8,128)(2,1)S(1)}, bf16[512,256]{1,0:T(8,128)(2,1)S(1)}) custom-call(s32[32]{0:T(128)S(1)} %copy-done.1, bf16[2,512,128]{2,1,0:T(8,128)(2,1)S(1)} %bitcast.28, bf16[2,512,128]{2,1,0:T(8,128)(2,1)S(1)} %bitcast.32, ...), custom_call_target="tpu_custom_call" | custom-call | flops 4026531840 | bytes 6291456 | tf_op jit(solution)/shard_map/attention_far/pallas_call | solution.py:247
  47.8 0.1 collective-permute-start.11
  47.9 1.8 %collective-permute-start.12 = (bf16[512,256]{1,0:T(8,128)(2,1)S(1)}, bf16[512,256]{1,0:T(8,128)(2,1)S(1)}, u32[]{:S(2)}, u32[]{:S(2)}) collective-permute-start(bf16[512,256]{1,0:T(8,128)(2,1)S(1)} %get-tuple-element.42), channel_id=1, source_target_pairs={{0,192},{16,208},{32,224},{48,240},{64,128},{80,144},{96,160},{112... | collective-permute-start | bytes 786440 | tf_op jit(solution)/shard_map/ppermute | solution.py:475
  49.8 1.7 %collective-permute-start.10 = (bf16[512,256]{1,0:T(8,128)(2,1)S(1)}, bf16[512,256]{1,0:T(8,128)(2,1)S(1)}, u32[]{:S(2)}, u32[]{:S(2)}) collective-permute-start(bf16[512,256]{1,0:T(8,128)(2,1)S(1)} %get-tuple-element.36), channel_id=1, source_target_pairs={{0,64},{16,80},{32,96},{48,112},{64,0},{80,16},{96,32},{112,48},{1... | collective-permute-start | bytes 786440 | tf_op jit(solution)/shard_map/ppermute | solution.py:475
  51.4 0.0 all-to-all-done.in_ref
  51.4 10.6 %experts.1 = bf16[16,160,128]{2,1,0:T(8,128)(2,1)} custom-call(bf16[16,320,128]{2,1,0:T(8,128)(2,1)} %all-to-all-done.in_ref, bf16[1,2048,768]{2,1,0:T(8,128)(2,1)} %rest_0_.1, bf16[1,2048,768]{2,1,0:T(8,128)(2,1)} %rest_1_.1, bf16[1,768,2048]{2,1,0:T(8,128)(2,1)} %rest_2_.1), custom_call_target="tpu_custom_call" | custom-call | flops 2516582400 | bytes 11534336 | tf_op jit(solution)/shard_map/experts/pallas_call | solution.py:391
  62.1 8.1 %all-to-all-start.1 = ((bf16[16,160,128]{2,1,0:T(8,128)(2,1)}), bf16[16,160,128]{2,1,0:T(8,128)(2,1)S(1)}, u32[]{:S(2)}, u32[]{:S(2)}) async-start(bf16[16,160,128]{2,1,0:T(8,128)(2,1)} %experts.1), calls=%async_computation.1 | async-start | bytes 1310720 | tf_op jit(solution)/shard_map/all_to_all | solution.py:511
  70.2 0.0 copy-start
  70.2 0.0 collective-permute-done.11
  70.2 0.0 collective-permute-done.12
  70.2 0.0 collective-permute-done.10
  70.2 0.1 convert_add_fusion
  70.4 2.0 %collective-permute-start.13 = (bf16[128,256]{1,0:T(8,128)(2,1)S(1)}, bf16[128,256]{1,0:T(8,128)(2,1)S(1)}, u32[]{:S(2)}, u32[]{:S(2)}) collective-permute-start(bf16[128,256]{1,0:T(8,128)(2,1)S(1)} %get-tuple-element.52), channel_id=1, source_target_pairs={{0,32},{16,48},{32,0},{48,16},{64,96},{80,112},{96,64},{112,80},{1... | collective-permute-start | bytes 196616 | tf_op jit(solution)/shard_map/ppermute | solution.py:475
  72.4 0.0 collective-permute-start.15
  72.4 1.7 %collective-permute-start.14 = (bf16[128,256]{1,0:T(8,128)(2,1)S(1)}, bf16[128,256]{1,0:T(8,128)(2,1)S(1)}, u32[]{:S(2)}, u32[]{:S(2)}) collective-permute-start(bf16[128,256]{1,0:T(8,128)(2,1)S(1)} %get-tuple-element.54), channel_id=1, source_target_pairs={{0,16},{16,0},{32,48},{48,32},{64,80},{80,64},{96,112},{112,96},{1... | collective-permute-start | bytes 196616 | tf_op jit(solution)/shard_map/ppermute | solution.py:475
  74.1 0.0 collective-permute-start.9
  74.1 2.4 %collective-permute-done.13 = bf16[128,256]{1,0:T(8,128)(2,1)S(1)} collective-permute-done((bf16[128,256]{1,0:T(8,128)(2,1)S(1)}, bf16[128,256]{1,0:T(8,128)(2,1)S(1)}, u32[]{:S(2)}, u32[]{:S(2)}) %collective-permute-start.13) | collective-permute-done | bytes 65568 | tf_op jit(solution)/shard_map/ppermute | solution.py:475
  76.6 1.9 %collective-permute-done.15 = bf16[128,256]{1,0:T(8,128)(2,1)S(1)} collective-permute-done((bf16[128,256]{1,0:T(8,128)(2,1)S(1)}, bf16[128,256]{1,0:T(8,128)(2,1)S(1)}, u32[]{:S(2)}, u32[]{:S(2)}) %collective-permute-start.15) | collective-permute-done | bytes 65568 | tf_op jit(solution)/shard_map/ppermute | solution.py:475
  78.4 0.0 collective-permute-done.14
  78.5 0.7 copy.22
  79.2 0.7 copy.21
  79.9 0.0 collective-permute-done.9
  80.0 0.9 pad_maximum_fusion
  80.9 8.5 %all-to-all-done.1.back_ref = bf16[16,160,128]{2,1,0:T(8,128)(2,1)S(1)} async-done(((bf16[16,160,128]{2,1,0:T(8,128)(2,1)}), bf16[16,160,128]{2,1,0:T(8,128)(2,1)S(1)}, u32[]{:S(2)}, u32[]{:S(2)}) %all-to-all-start.1) | async-done | bytes 655392 | tf_op jit(solution)/shard_map/all_to_all | solution.py:511
  89.4 0.0 copy-done
  89.4 1.5 %combine.1 = bf16[128,2048]{1,0:T(8,128)(2,1)} custom-call(f32[160,128]{1,0:T(8,128)S(1)} %copy-done, bf16[16,160,128]{2,1,0:T(8,128)(2,1)S(1)} %all-to-all-done.1.back_ref), custom_call_target="tpu_custom_call" | custom-call | tf_op jit(solution)/shard_map/combine/pallas_call | solution.py:437
  (15 shorter events, 0.4 us)
Async XLA Ops:
  0.6 13.3 %copy-start.5 = (bf16[128,2,128]{2,1,0:T(2,128)(2,1)S(1)}, bf16[128,2,128]{2,1,0:T(2,128)(2,1)}, u32[]{:S(2)}) copy-start(bf16[128,2,128]{2,1,0:T(2,128)(2,1)} %param.17) | copy-start | bytes 196612
  0.6 13.2 %copy-start.4 = (bf16[128,2,128]{2,1,0:T(2,128)(2,1)S(1)}, bf16[128,2,128]{2,1,0:T(2,128)(2,1)}, u32[]{:S(2)}) copy-start(bf16[128,2,128]{2,1,0:T(2,128)(2,1)} %param.16) | copy-start | bytes 196612
  0.7 20.8 %copy-start.6 = (f32[128,16]{0,1:T(8,128)S(1)}, f32[128,16]{0,1:T(8,128)}, u32[]{:S(2)}) copy-start(f32[128,16]{0,1:T(8,128)} %param.20) | copy-start | bytes 24580
  0.7 20.8 %copy-start.7 = (f32[128,16]{0,1:T(8,128)S(1)}, f32[128,16]{0,1:T(8,128)}, u32[]{:S(2)}) copy-start(f32[128,16]{0,1:T(8,128)} %param.19) | copy-start | bytes 24580
  0.7 21.5 %copy-start.3 = (bf16[128,16,128]{2,1,0:T(8,128)(2,1)S(1)}, bf16[128,16,128]{2,1,0:T(8,128)(2,1)}, u32[]{:S(2)}) copy-start(bf16[128,16,128]{2,1,0:T(8,128)(2,1)} %param.18) | copy-start | bytes 1572868
  0.7 20.9 %copy-start.2 = (bf16[128,16,128]{2,1,0:T(8,128)(2,1)S(1)}, bf16[128,16,128]{2,1,0:T(8,128)(2,1)}, u32[]{:S(2)}) copy-start(bf16[128,16,128]{2,1,0:T(8,128)(2,1)} %param.15) | copy-start | bytes 1572868
  4.6 22.0 %copy-start.1 = (s32[32]{0:T(128)S(1)}, s32[32]{0:T(128)}, u32[]{:S(2)}) copy-start(s32[32]{0:T(128)} %span_ref.3) | copy-start | bytes 388
  4.6 46.8 %all-to-all-start = ((bf16[16,320,128]{2,1,0:T(8,128)(2,1)}), bf16[16,320,128]{2,1,0:T(8,128)(2,1)}, u32[]{:S(2)}, u32[]{:S(2)}) async-start(bf16[16,320,128]{2,1,0:T(8,128)(2,1)} %get-tuple-element.35), calls=%async_computation | async-start | bytes 2621440 | tf_op jit(solution)/shard_map/all_to_all | solution.py:486
  14.0 1.3 %collective-permute-start.4 = (bf16[128,256]{1,0:T(8,128)(2,1)S(1)}, bf16[128,256]{1,0:T(8,128)(2,1)S(1)}, u32[]{:S(2)}, u32[]{:S(2)}) collective-permute-start(bf16[128,256]{1,0:T(8,128)(2,1)S(1)} %select_bitcast_fusion.2), channel_id=1, source_target_pairs={{0,16},{16,0},{32,48},{48,32},{64,80},{80,64},{96,112},{112,96},{1... | collective-permute-start | bytes 196616 | tf_op jit(solution)/shard_map/ppermute | solution.py:475
  14.1 8.3 %collective-permute-start.5 = (bf16[128,256]{1,0:T(8,128)(2,1)S(1)}, bf16[128,256]{1,0:T(8,128)(2,1)S(1)}, u32[]{:S(2)}, u32[]{:S(2)}) collective-permute-start(bf16[128,256]{1,0:T(8,128)(2,1)S(1)} %select_bitcast_fusion.2), channel_id=1, source_target_pairs={{0,48},{16,32},{32,16},{48,0},{64,112},{80,96},{96,80},{112,64},{1... | collective-permute-start | bytes 196616 | tf_op jit(solution)/shard_map/ppermute | solution.py:475
  15.3 6.1 %collective-permute-start = (bf16[128,256]{1,0:T(8,128)(2,1)S(1)}, bf16[128,256]{1,0:T(8,128)(2,1)S(1)}, u32[]{:S(2)}, u32[]{:S(2)}) collective-permute-start(bf16[128,256]{1,0:T(8,128)(2,1)S(1)} %get-tuple-element.51), channel_id=1, source_target_pairs={{0,32},{16,48},{32,0},{48,16},{64,96},{80,112},{96,64},{112,80},{1... | collective-permute-start | bytes 196616 | tf_op jit(solution)/shard_map/ppermute | solution.py:475
  21.5 4.7 %collective-permute-start.3 = (f32[2,8,128]{2,1,0:T(8,128)S(1)}, f32[2,8,128]{2,1,0:T(8,128)S(1)}, u32[]{:S(2)}, u32[]{:S(2)}) collective-permute-start(f32[2,8,128]{2,1,0:T(8,128)S(1)} %get-tuple-element.65), channel_id=1, source_target_pairs={{0,16},{16,0},{32,48},{48,32},{64,80},{80,64},{96,112},{112,96},{1... | collective-permute-start | bytes 24584 | tf_op jit(solution)/shard_map/ppermute | solution.py:475
  21.6 5.0 %collective-permute-start.1 = (bf16[128,8,128]{2,1,0:T(8,128)(2,1)S(1)}, bf16[128,8,128]{2,1,0:T(8,128)(2,1)S(1)}, u32[]{:S(2)}, u32[]{:S(2)}) collective-permute-start(bf16[128,8,128]{2,1,0:T(8,128)(2,1)S(1)} %get-tuple-element.59), channel_id=1, source_target_pairs={{0,16},{16,0},{32,48},{48,32},{64,80},{80,64},{96,112},{112,96},{1... | collective-permute-start | bytes 786440 | tf_op jit(solution)/shard_map/ppermute | solution.py:475
  22.2 4.4 %collective-permute-start.2 = (bf16[128,8,128]{2,1,0:T(8,128)(2,1)S(1)}, bf16[128,8,128]{2,1,0:T(8,128)(2,1)S(1)}, u32[]{:S(2)}, u32[]{:S(2)}) collective-permute-start(bf16[128,8,128]{2,1,0:T(8,128)(2,1)S(1)} %get-tuple-element.57), channel_id=1, source_target_pairs={{0,16},{16,0},{32,48},{48,32},{64,80},{80,64},{96,112},{112,96},{1... | collective-permute-start | bytes 786440 | tf_op jit(solution)/shard_map/ppermute | solution.py:475
  22.4 15.7 %collective-permute-start.8 = (bf16[512,256]{1,0:T(8,128)(2,1)S(1)}, bf16[512,256]{1,0:T(8,128)(2,1)S(1)}, u32[]{:S(2)}, u32[]{:S(2)}) collective-permute-start(bf16[512,256]{1,0:T(8,128)(2,1)S(1)} %pad_maximum_fusion.1.kv_ref), channel_id=1, source_target_pairs={{0,192},{16,208},{32,224},{48,240},{64,128},{80,144},{96,160},{112... | collective-permute-start | bytes 786440 | tf_op jit(solution)/shard_map/ppermute | solution.py:475
  25.5 12.6 %collective-permute-start.7 = (bf16[512,256]{1,0:T(8,128)(2,1)S(1)}, bf16[512,256]{1,0:T(8,128)(2,1)S(1)}, u32[]{:S(2)}, u32[]{:S(2)}) collective-permute-start(bf16[512,256]{1,0:T(8,128)(2,1)S(1)} %pad_maximum_fusion.1.kv_ref), channel_id=1, source_target_pairs={{0,128},{16,144},{32,160},{48,176},{64,192},{80,208},{96,224},{112... | collective-permute-start | bytes 786440 | tf_op jit(solution)/shard_map/ppermute | solution.py:475
  26.1 12.7 %collective-permute-start.6 = (bf16[512,256]{1,0:T(8,128)(2,1)S(1)}, bf16[512,256]{1,0:T(8,128)(2,1)S(1)}, u32[]{:S(2)}, u32[]{:S(2)}) collective-permute-start(bf16[512,256]{1,0:T(8,128)(2,1)S(1)} %pad_maximum_fusion.1.kv_ref), channel_id=1, source_target_pairs={{0,64},{16,80},{32,96},{48,112},{64,0},{80,16},{96,32},{112,48},{1... | collective-permute-start | bytes 786440 | tf_op jit(solution)/shard_map/ppermute | solution.py:475
  47.8 22.4 %collective-permute-start.11 = (bf16[512,256]{1,0:T(8,128)(2,1)S(1)}, bf16[512,256]{1,0:T(8,128)(2,1)S(1)}, u32[]{:S(2)}, u32[]{:S(2)}) collective-permute-start(bf16[512,256]{1,0:T(8,128)(2,1)S(1)} %get-tuple-element.41), channel_id=1, source_target_pairs={{0,128},{16,144},{32,160},{48,176},{64,192},{80,208},{96,224},{112... | collective-permute-start | bytes 786440 | tf_op jit(solution)/shard_map/ppermute | solution.py:475
  47.9 22.3 %collective-permute-start.12 = (bf16[512,256]{1,0:T(8,128)(2,1)S(1)}, bf16[512,256]{1,0:T(8,128)(2,1)S(1)}, u32[]{:S(2)}, u32[]{:S(2)}) collective-permute-start(bf16[512,256]{1,0:T(8,128)(2,1)S(1)} %get-tuple-element.42), channel_id=1, source_target_pairs={{0,192},{16,208},{32,224},{48,240},{64,128},{80,144},{96,160},{112... | collective-permute-start | bytes 786440 | tf_op jit(solution)/shard_map/ppermute | solution.py:475
  49.8 20.5 %collective-permute-start.10 = (bf16[512,256]{1,0:T(8,128)(2,1)S(1)}, bf16[512,256]{1,0:T(8,128)(2,1)S(1)}, u32[]{:S(2)}, u32[]{:S(2)}) collective-permute-start(bf16[512,256]{1,0:T(8,128)(2,1)S(1)} %get-tuple-element.36), channel_id=1, source_target_pairs={{0,64},{16,80},{32,96},{48,112},{64,0},{80,16},{96,32},{112,48},{1... | collective-permute-start | bytes 786440 | tf_op jit(solution)/shard_map/ppermute | solution.py:475
  62.1 27.3 %all-to-all-start.1 = ((bf16[16,160,128]{2,1,0:T(8,128)(2,1)}), bf16[16,160,128]{2,1,0:T(8,128)(2,1)S(1)}, u32[]{:S(2)}, u32[]{:S(2)}) async-start(bf16[16,160,128]{2,1,0:T(8,128)(2,1)} %experts.1), calls=%async_computation.1 | async-start | bytes 1310720 | tf_op jit(solution)/shard_map/all_to_all | solution.py:511
  70.2 19.2 %copy-start = (f32[160,128]{1,0:T(8,128)S(1)}, f32[160,128]{1,0:T(8,128)}, u32[]{:S(2)}) copy-start(f32[160,128]{1,0:T(8,128)} %get-tuple-element.43.weight_ref) | copy-start | bytes 245764
  70.4 6.2 %collective-permute-start.13 = (bf16[128,256]{1,0:T(8,128)(2,1)S(1)}, bf16[128,256]{1,0:T(8,128)(2,1)S(1)}, u32[]{:S(2)}, u32[]{:S(2)}) collective-permute-start(bf16[128,256]{1,0:T(8,128)(2,1)S(1)} %get-tuple-element.52), channel_id=1, source_target_pairs={{0,32},{16,48},{32,0},{48,16},{64,96},{80,112},{96,64},{112,80},{1... | collective-permute-start | bytes 196616 | tf_op jit(solution)/shard_map/ppermute | solution.py:475
  72.4 6.0 %collective-permute-start.15 = (bf16[128,256]{1,0:T(8,128)(2,1)S(1)}, bf16[128,256]{1,0:T(8,128)(2,1)S(1)}, u32[]{:S(2)}, u32[]{:S(2)}) collective-permute-start(bf16[128,256]{1,0:T(8,128)(2,1)S(1)} %get-tuple-element.53), channel_id=1, source_target_pairs={{0,48},{16,32},{32,16},{48,0},{64,112},{80,96},{96,80},{112,64},{1... | collective-permute-start | bytes 196616 | tf_op jit(solution)/shard_map/ppermute | solution.py:475
  72.4 6.0 %collective-permute-start.14 = (bf16[128,256]{1,0:T(8,128)(2,1)S(1)}, bf16[128,256]{1,0:T(8,128)(2,1)S(1)}, u32[]{:S(2)}, u32[]{:S(2)}) collective-permute-start(bf16[128,256]{1,0:T(8,128)(2,1)S(1)} %get-tuple-element.54), channel_id=1, source_target_pairs={{0,16},{16,0},{32,48},{48,32},{64,80},{80,64},{96,112},{112,96},{1... | collective-permute-start | bytes 196616 | tf_op jit(solution)/shard_map/ppermute | solution.py:475
  74.1 5.8 %collective-permute-start.9 = (bf16[2,512,128]{2,1,0:T(8,128)(2,1)S(1)}, bf16[2,512,128]{2,1,0:T(8,128)(2,1)S(1)}, u32[]{:S(2)}, u32[]{:S(2)}) collective-permute-start(bf16[2,512,128]{2,1,0:T(8,128)(2,1)S(1)} %get-tuple-element.38), channel_id=1, source_target_pairs={{0,16},{16,0},{32,48},{48,32},{64,80},{80,64},{96,112},{112,96},{1... | collective-permute-start | bytes 786440 | tf_op jit(solution)/shard_map/ppermute | solution.py:475

commit v2 on v1

--- a/solution.py
+++ b/solution.py
@@ -474,15 +474,16 @@
     chips = members // 2
     trade = lambda array, k: lax.ppermute(array, "ctx", [(i, i ^ k) for i in range(members)])
 
-    send, weight = dispatch(expert_ids, keep_mask, route_weight, moe_input, moe_grad, experts)
-    send, key_tensor, value_tensor = lax.optimization_barrier((send, key_tensor, value_tensor))
     kv = jnp.concatenate([key_tensor, value_tensor], axis=2)
     kv_own = jnp.where(first, kv[:, 0], kv[:, 1])
     kv_away = jnp.where(first, kv[:, 1], kv[:, 0])
+    kv_own, kv_away, expert_ids = lax.optimization_barrier((kv_own, kv_away, expert_ids))
     kv_got = trade(kv_away, 1)
     kv_near, kv_cross = trade(kv_own, 2), trade(kv_away, 3)
+    send, weight = dispatch(expert_ids, keep_mask, route_weight, moe_input, moe_grad, experts)
     ordered = lambda mine, other: [jnp.where(first, mine, other), jnp.where(first, other, mine)]
     kv_pair = jnp.concatenate(ordered(kv_own, kv_got) + ordered(kv_near, kv_cross), axis=0)
+    send, kv_pair = lax.optimization_barrier((send, kv_pair))
     received = lax.all_to_all(send, "exp", split_axis=0, concat_axis=0, tiled=True)
     kv_list = [trade(kv_pair, 4 * k) for k in range(1, chips // 2)]
 

time: 92.1 us -> 90.6 us (0.984)
  Pallas kernels: 28.5 us -> 24.8 us
  local copies, waits for them, and re-layouts: 1.47 us -> 3.23 us
    ppermute x16, waiting for transfers between devices: 17 us -> 12.1 us  [on_device(): lax.ppermute(array, 'ctx', [(i, i ^ k) for i in range(members)])]
    ppermute x16, starting transfers between devices: 15.8 us -> 20.1 us  [on_device(): lax.ppermute(array, 'ctx', [(i, i ^ k) for i in range(members)])]
    all_to_all x1, starting transfers between devices: 8.11 us -> 4.16 us  [on_device(): lax.all_to_all(slot_grad, 'exp', split_axis=0, concat_axis=0, tiled=True)]
    all_to_all x1, waiting for transfers between devices: 0.01 us -> 3.92 us  [on_device(): lax.all_to_all(send, 'exp', split_axis=0, concat_axis=0, tiled=True)]
    pallas_call x1, Pallas kernels: 9.02 us -> 5.42 us  [attention_far(): pl.pallas_call(functools.partial(far_kernel, scale, blocks), out_shape=(j...]
    all_to_all x1, waiting for transfers between devices: 8.49 us -> 9.64 us  [on_device(): lax.all_to_all(slot_grad, 'exp', split_axis=0, concat_axis=0, tiled=True)]
    unnamed x19 -> x15, local copies, waits for them, and re-layouts: 1.44 us -> 2.36 us
  transfers between devices with their start and end apart: 18 -> 18, of which waited for: 7 -> 6; matrix products, arithmetic and copies ran while one was open for 3% -> 3% of each run, Pallas kernels for 25% -> 26%
where the time goes in v2:
time: 90.6 us; the launch traced here: 88.8 us
  starting transfers between devices  33 us (36%)
  waiting for transfers between devices  25.7 us (28%)
  Pallas kernels  24.8 us (27%)
  local copies, waits for them, and re-layouts  3.23 us (4%)
  other arithmetic  1.31 us (1%)
  between operations  0.91 us (1%)
    ppermute x16, starting transfers between devices, on_device(): lax.ppermute(array, 'ctx', [(i, i ^ k) for i in range(members)])  20.1 us
    ppermute x16, waiting for transfers between devices, on_device(): lax.ppermute(array, 'ctx', [(i, i ^ k) for i in range(members)])  12.1 us
    pallas_call x1, Pallas kernels, mlp(): pl.pallas_call(mlp_kernel, out_shape=jax.ShapeDtypeStruct((sources, block...  10.6 us
    all_to_all x1, waiting for transfers between devices, on_device(): lax.all_to_all(slot_grad, 'exp', split_axis=0, concat_axis=0, tiled=True)  9.64 us
    all_to_all x1, starting transfers between devices, on_device(): lax.all_to_all(send, 'exp', split_axis=0, concat_axis=0, tiled=True)  8.69 us
    pallas_call x1, Pallas kernels, attention_far(): pl.pallas_call(functools.partial(far_kernel, scale, blocks), out_shape=(j...  5.42 us
    all_to_all x1, starting transfers between devices, on_device(): lax.all_to_all(slot_grad, 'exp', split_axis=0, concat_axis=0, tiled=True)  4.16 us
    all_to_all x1, waiting for transfers between devices, on_device(): lax.all_to_all(send, 'exp', split_axis=0, concat_axis=0, tiled=True)  3.92 us
  transfers between devices with their start and end apart: 18, of which 6 were waited for; matrix products, arithmetic and copies ran while one was open for 3% of the time, Pallas kernels for 26%

profile of v2, /device:TPU:4, one launch (start us, length us, event | category | flops | bytes accessed | tf_op | source)
XLA Modules:
  0.0 88.8 jit_solution(11730485222017092927)
XLA Ops:
  0.6 0.0 copy-start.2
  0.6 0.0 copy-start.3
  0.7 0.9 %copy_dynamic-update-slice_fusion.1 = bf16[128,2,256]{2,0,1:T(8,128)(2,1)S(1)} fusion(bf16[128,2,128]{2,1,0:T(2,128)(2,1)} %param.16), kind=kLoop, calls=%fused_computation.19 | loop fusion | bytes 131072
  1.6 0.9 copy_dynamic-update-slice_fusion
  2.5 0.1 collective-permute-start.4
  2.6 2.4 %collective-permute-start.5 = (bf16[128,256]{1,0:T(8,128)(2,1)S(1)}, bf16[128,256]{1,0:T(8,128)(2,1)S(1)}, u32[]{:S(2)}, u32[]{:S(2)}) collective-permute-start(bf16[128,256]{1,0:T(8,128)(2,1)S(1)} %get-tuple-element.33), channel_id=1, source_target_pairs={{0,48},{16,32},{32,16},{48,0},{64,112},{80,96},{96,80},{112,64},{1... | collective-permute-start | bytes 196616 | tf_op jit(solution)/shard_map/ppermute | solution.py:475
  5.0 1.3 %collective-permute-start = (bf16[128,256]{1,0:T(8,128)(2,1)S(1)}, bf16[128,256]{1,0:T(8,128)(2,1)S(1)}, u32[]{:S(2)}, u32[]{:S(2)}) collective-permute-start(bf16[128,256]{1,0:T(8,128)(2,1)S(1)} %get-tuple-element.26), channel_id=1, source_target_pairs={{0,32},{16,48},{32,0},{48,16},{64,96},{80,112},{96,64},{112,80},{1... | collective-permute-start | bytes 196616 | tf_op jit(solution)/shard_map/ppermute | solution.py:475
  6.2 3.8 %dispatch.1 = (bf16[16,320,128]{2,1,0:T(8,128)(2,1)}, f32[160,128]{1,0:T(8,128)}) custom-call(s32[8,128]{1,0:T(8,128)} %bitcast.39, s32[8,128]{1,0:T(8,128)} %bitcast.40, f32[8,128]{1,0:T(8,128)} %bitcast.41, bf16[128,2048]{1,0:T(8,128)(2,1)} %x_hbm.1, bf16[128,2048]{1,0:T(8,128)(2,1)} %g_hbm.1), custom_call_target="tpu_custom_call" | custom-call | tf_op jit(solution)/shard_map/dispatch/pallas_call | solution.py:322
  10.1 0.0 copy-start.4
  10.1 0.0 copy-start.5
  10.1 0.0 copy-start.1
  10.1 0.0 collective-permute-done.4
  10.1 0.6 collective-permute-done
  10.7 0.0 collective-permute-done.5
  10.8 8.7 %all-to-all-start = ((bf16[16,320,128]{2,1,0:T(8,128)(2,1)}), bf16[16,320,128]{2,1,0:T(8,128)(2,1)}, u32[]{:S(2)}, u32[]{:S(2)}) async-start(bf16[16,320,128]{2,1,0:T(8,128)(2,1)} %get-tuple-element.39), calls=%async_computation | async-start | bytes 2621440 | tf_op jit(solution)/shard_map/all_to_all | solution.py:487
  19.5 0.0 copy-done.2
  19.5 0.1 collective-permute-start.1
  19.6 0.0 copy-done.3
  19.7 0.6 collective-permute-start.2
  20.3 0.0 copy-done.4
  20.3 0.0 copy-done.5
  20.3 0.1 collective-permute-start.3
  20.4 3.1 %collective-permute-start.8 = (bf16[512,256]{1,0:T(8,128)(2,1)S(1)}, bf16[512,256]{1,0:T(8,128)(2,1)S(1)}, u32[]{:S(2)}, u32[]{:S(2)}) collective-permute-start(bf16[512,256]{1,0:T(8,128)(2,1)S(1)} %pad_maximum_fusion.1.kv_ref), channel_id=1, source_target_pairs={{0,192},{16,208},{32,224},{48,240},{64,128},{80,144},{96,160},{112... | collective-permute-start | bytes 786440 | tf_op jit(solution)/shard_map/ppermute | solution.py:475
  23.5 0.6 collective-permute-start.7
  24.1 0.0 collective-permute-done.3
  24.1 0.4 collective-permute-start.6
  24.6 0.0 collective-permute-done.1
  24.6 0.0 collective-permute-done.2
  24.6 0.0 copy-done.1
  24.6 3.4 %attention_near.1 = (f32[4,128,512]{2,1,0:T(8,128)S(1)}, f32[512,256]{1,0:T(8,128)S(1)}, f32[4,1024]{1,0:T(4,128)S(1)}) custom-call(s32[32]{0:T(128)S(1)} %copy-done.1, bf16[2,512,128]{2,1,0:T(8,128)(2,1)S(1)} %bitcast.26, bf16[2,512,128]{2,1,0:T(8,128)(2,1)S(1)} %bitcast.30, bf16[2,512,128]{2,1,0:T(8,128)(2,1)S(1)} %bitcast.28, ...), custom_call_target="tpu_custom_call" | custom-call | flops 1342177280 | bytes 3145728 | tf_op jit(solution)/shard_map/attention_near/pallas_call | solution.py:220
  28.0 8.0 %collective-permute-done.8.rest_2_ = bf16[512,256]{1,0:T(8,128)(2,1)S(1)} collective-permute-done((bf16[512,256]{1,0:T(8,128)(2,1)S(1)}, bf16[512,256]{1,0:T(8,128)(2,1)S(1)}, u32[]{:S(2)}, u32[]{:S(2)}) %collective-permute-start.8) | collective-permute-done | bytes 262176 | tf_op jit(solution)/shard_map/ppermute | solution.py:475
  36.0 0.0 collective-permute-done.7.rest_1_
  36.0 0.6 collective-permute-done.6.rest_0_
  36.6 5.4 %attention_far.1 = (bf16[2,512,128]{2,1,0:T(8,128)(2,1)S(1)}, bf16[2,512,128]{2,1,0:T(8,128)(2,1)S(1)}, bf16[512,256]{1,0:T(8,128)(2,1)S(1)}, bf16[512,256]{1,0:T(8,128)(2,1)S(1)}, bf16[512,256]{1,0:T(8,128)(2,1)S(1)}) custom-call(s32[32]{0:T(128)S(1)} %copy-done.1, bf16[2,512,128]{2,1,0:T(8,128)(2,1)S(1)} %bitcast.27, bf16[2,512,128]{2,1,0:T(8,128)(2,1)S(1)} %bitcast.31, ...), custom_call_target="tpu_custom_call" | custom-call | flops 4026531840 | bytes 6291456 | tf_op jit(solution)/shard_map/attention_far/pallas_call | solution.py:247
  42.0 5.1 %collective-permute-start.11 = (bf16[512,256]{1,0:T(8,128)(2,1)S(1)}, bf16[512,256]{1,0:T(8,128)(2,1)S(1)}, u32[]{:S(2)}, u32[]{:S(2)}) collective-permute-start(bf16[512,256]{1,0:T(8,128)(2,1)S(1)} %get-tuple-element.45), channel_id=1, source_target_pairs={{0,128},{16,144},{32,160},{48,176},{64,192},{80,208},{96,224},{112... | collective-permute-start | bytes 786440 | tf_op jit(solution)/shard_map/ppermute | solution.py:475
  47.1 2.1 %collective-permute-start.12 = (bf16[512,256]{1,0:T(8,128)(2,1)S(1)}, bf16[512,256]{1,0:T(8,128)(2,1)S(1)}, u32[]{:S(2)}, u32[]{:S(2)}) collective-permute-start(bf16[512,256]{1,0:T(8,128)(2,1)S(1)} %get-tuple-element.46), channel_id=1, source_target_pairs={{0,192},{16,208},{32,224},{48,240},{64,128},{80,144},{96,160},{112... | collective-permute-start | bytes 786440 | tf_op jit(solution)/shard_map/ppermute | solution.py:475
  49.2 0.5 collective-permute-start.10
  49.7 3.9 %all-to-all-done.in_ref = bf16[16,320,128]{2,1,0:T(8,128)(2,1)} async-done(((bf16[16,320,128]{2,1,0:T(8,128)(2,1)}), bf16[16,320,128]{2,1,0:T(8,128)(2,1)}, u32[]{:S(2)}, u32[]{:S(2)}) %all-to-all-start) | async-done | bytes 1310752 | tf_op jit(solution)/shard_map/all_to_all | solution.py:487
  53.6 10.6 %experts.1 = bf16[16,160,128]{2,1,0:T(8,128)(2,1)} custom-call(bf16[16,320,128]{2,1,0:T(8,128)(2,1)} %all-to-all-done.in_ref, bf16[1,2048,768]{2,1,0:T(8,128)(2,1)} %rest_0_.1, bf16[1,2048,768]{2,1,0:T(8,128)(2,1)} %rest_1_.1, bf16[1,768,2048]{2,1,0:T(8,128)(2,1)} %rest_2_.1), custom_call_target="tpu_custom_call" | custom-call | flops 2516582400 | bytes 11534336 | tf_op jit(solution)/shard_map/experts/pallas_call | solution.py:391
  64.3 4.2 %all-to-all-start.1 = ((bf16[16,160,128]{2,1,0:T(8,128)(2,1)}), bf16[16,160,128]{2,1,0:T(8,128)(2,1)S(1)}, u32[]{:S(2)}, u32[]{:S(2)}) async-start(bf16[16,160,128]{2,1,0:T(8,128)(2,1)} %experts.1), calls=%async_computation.1 | async-start | bytes 1310720 | tf_op jit(solution)/shard_map/all_to_all | solution.py:512
  68.4 0.0 copy-start
  68.5 0.0 collective-permute-done.11
  68.5 0.0 collective-permute-done.12
  68.5 0.0 collective-permute-done.10
  68.5 0.1 convert_add_fusion
  68.6 0.4 collective-permute-start.13
  69.0 1.2 %collective-permute-start.15 = (bf16[128,256]{1,0:T(8,128)(2,1)S(1)}, bf16[128,256]{1,0:T(8,128)(2,1)S(1)}, u32[]{:S(2)}, u32[]{:S(2)}) collective-permute-start(bf16[128,256]{1,0:T(8,128)(2,1)S(1)} %get-tuple-element.55), channel_id=1, source_target_pairs={{0,48},{16,32},{32,16},{48,0},{64,112},{80,96},{96,80},{112,64},{1... | collective-permute-start | bytes 196616 | tf_op jit(solution)/shard_map/ppermute | solution.py:475
  70.2 2.2 %collective-permute-start.14 = (bf16[128,256]{1,0:T(8,128)(2,1)S(1)}, bf16[128,256]{1,0:T(8,128)(2,1)S(1)}, u32[]{:S(2)}, u32[]{:S(2)}) collective-permute-start(bf16[128,256]{1,0:T(8,128)(2,1)S(1)} %get-tuple-element.56), channel_id=1, source_target_pairs={{0,16},{16,0},{32,48},{48,32},{64,80},{80,64},{96,112},{112,96},{1... | collective-permute-start | bytes 196616 | tf_op jit(solution)/shard_map/ppermute | solution.py:475
  72.4 0.0 collective-permute-start.9
  72.4 2.8 %collective-permute-done.13 = bf16[128,256]{1,0:T(8,128)(2,1)S(1)} collective-permute-done((bf16[128,256]{1,0:T(8,128)(2,1)S(1)}, bf16[128,256]{1,0:T(8,128)(2,1)S(1)}, u32[]{:S(2)}, u32[]{:S(2)}) %collective-permute-start.13) | collective-permute-done | bytes 65568 | tf_op jit(solution)/shard_map/ppermute | solution.py:475
  75.2 0.0 collective-permute-done.15
  75.2 0.0 collective-permute-done.14
  75.4 0.7 copy.22
  76.1 0.7 copy.21
  76.8 0.0 collective-permute-done.9
  76.8 0.9 pad_maximum_fusion
  77.7 9.6 %all-to-all-done.1.back_ref = bf16[16,160,128]{2,1,0:T(8,128)(2,1)S(1)} async-done(((bf16[16,160,128]{2,1,0:T(8,128)(2,1)}), bf16[16,160,128]{2,1,0:T(8,128)(2,1)S(1)}, u32[]{:S(2)}, u32[]{:S(2)}) %all-to-all-start.1) | async-done | bytes 655392 | tf_op jit(solution)/shard_map/all_to_all | solution.py:512
  87.3 0.0 copy-done
  87.3 1.5 %combine.1 = bf16[128,2048]{1,0:T(8,128)(2,1)} custom-call(f32[160,128]{1,0:T(8,128)S(1)} %copy-done, bf16[16,160,128]{2,1,0:T(8,128)(2,1)S(1)} %all-to-all-done.1.back_ref), custom_call_target="tpu_custom_call" | custom-call | tf_op jit(solution)/shard_map/combine/pallas_call | solution.py:437
  (12 shorter events, 0.3 us)
Async XLA Ops:
  0.6 18.8 %copy-start.2 = (bf16[128,16,128]{2,1,0:T(8,128)(2,1)S(1)}, bf16[128,16,128]{2,1,0:T(8,128)(2,1)}, u32[]{:S(2)}) copy-start(bf16[128,16,128]{2,1,0:T(8,128)(2,1)} %param.15) | copy-start | bytes 1572868
  0.6 19.0 %copy-start.3 = (bf16[128,16,128]{2,1,0:T(8,128)(2,1)S(1)}, bf16[128,16,128]{2,1,0:T(8,128)(2,1)}, u32[]{:S(2)}) copy-start(bf16[128,16,128]{2,1,0:T(8,128)(2,1)} %param.18) | copy-start | bytes 1572868
  2.5 7.6 %collective-permute-start.4 = (bf16[128,256]{1,0:T(8,128)(2,1)S(1)}, bf16[128,256]{1,0:T(8,128)(2,1)S(1)}, u32[]{:S(2)}, u32[]{:S(2)}) collective-permute-start(bf16[128,256]{1,0:T(8,128)(2,1)S(1)} %get-tuple-element.33), channel_id=1, source_target_pairs={{0,16},{16,0},{32,48},{48,32},{64,80},{80,64},{96,112},{112,96},{1... | collective-permute-start | bytes 196616 | tf_op jit(solution)/shard_map/ppermute | solution.py:475
  2.6 8.1 %collective-permute-start.5 = (bf16[128,256]{1,0:T(8,128)(2,1)S(1)}, bf16[128,256]{1,0:T(8,128)(2,1)S(1)}, u32[]{:S(2)}, u32[]{:S(2)}) collective-permute-start(bf16[128,256]{1,0:T(8,128)(2,1)S(1)} %get-tuple-element.33), channel_id=1, source_target_pairs={{0,48},{16,32},{32,16},{48,0},{64,112},{80,96},{96,80},{112,64},{1... | collective-permute-start | bytes 196616 | tf_op jit(solution)/shard_map/ppermute | solution.py:475
  5.0 5.8 %collective-permute-start = (bf16[128,256]{1,0:T(8,128)(2,1)S(1)}, bf16[128,256]{1,0:T(8,128)(2,1)S(1)}, u32[]{:S(2)}, u32[]{:S(2)}) collective-permute-start(bf16[128,256]{1,0:T(8,128)(2,1)S(1)} %get-tuple-element.26), channel_id=1, source_target_pairs={{0,32},{16,48},{32,0},{48,16},{64,96},{80,112},{96,64},{112,80},{1... | collective-permute-start | bytes 196616 | tf_op jit(solution)/shard_map/ppermute | solution.py:475
  10.1 10.2 %copy-start.4 = (f32[128,16]{0,1:T(8,128)S(1)}, f32[128,16]{0,1:T(8,128)}, u32[]{:S(2)}) copy-start(f32[128,16]{0,1:T(8,128)} %param.20) | copy-start | bytes 24580
  10.1 10.2 %copy-start.5 = (f32[128,16]{0,1:T(8,128)S(1)}, f32[128,16]{0,1:T(8,128)}, u32[]{:S(2)}) copy-start(f32[128,16]{0,1:T(8,128)} %param.19) | copy-start | bytes 24580
  10.1 14.5 %copy-start.1 = (s32[32]{0:T(128)S(1)}, s32[32]{0:T(128)}, u32[]{:S(2)}) copy-start(s32[32]{0:T(128)} %span_ref.3) | copy-start | bytes 388
  10.8 42.9 %all-to-all-start = ((bf16[16,320,128]{2,1,0:T(8,128)(2,1)}), bf16[16,320,128]{2,1,0:T(8,128)(2,1)}, u32[]{:S(2)}, u32[]{:S(2)}) async-start(bf16[16,320,128]{2,1,0:T(8,128)(2,1)} %get-tuple-element.39), calls=%async_computation | async-start | bytes 2621440 | tf_op jit(solution)/shard_map/all_to_all | solution.py:487
  19.5 5.0 %collective-permute-start.1 = (bf16[128,8,128]{2,1,0:T(8,128)(2,1)S(1)}, bf16[128,8,128]{2,1,0:T(8,128)(2,1)S(1)}, u32[]{:S(2)}, u32[]{:S(2)}) collective-permute-start(bf16[128,8,128]{2,1,0:T(8,128)(2,1)S(1)} %get-tuple-element.61), channel_id=1, source_target_pairs={{0,16},{16,0},{32,48},{48,32},{64,80},{80,64},{96,112},{112,96},{1... | collective-permute-start | bytes 786440 | tf_op jit(solution)/shard_map/ppermute | solution.py:475
  19.7 4.9 %collective-permute-start.2 = (bf16[128,8,128]{2,1,0:T(8,128)(2,1)S(1)}, bf16[128,8,128]{2,1,0:T(8,128)(2,1)S(1)}, u32[]{:S(2)}, u32[]{:S(2)}) collective-permute-start(bf16[128,8,128]{2,1,0:T(8,128)(2,1)S(1)} %get-tuple-element.59), channel_id=1, source_target_pairs={{0,16},{16,0},{32,48},{48,32},{64,80},{80,64},{96,112},{112,96},{1... | collective-permute-start | bytes 786440 | tf_op jit(solution)/shard_map/ppermute | solution.py:475
  20.3 3.8 %collective-permute-start.3 = (f32[2,8,128]{2,1,0:T(8,128)S(1)}, f32[2,8,128]{2,1,0:T(8,128)S(1)}, u32[]{:S(2)}, u32[]{:S(2)}) collective-permute-start(f32[2,8,128]{2,1,0:T(8,128)S(1)} %get-tuple-element.71), channel_id=1, source_target_pairs={{0,16},{16,0},{32,48},{48,32},{64,80},{80,64},{96,112},{112,96},{1... | collective-permute-start | bytes 24584 | tf_op jit(solution)/shard_map/ppermute | solution.py:475
  20.4 15.6 %collective-permute-start.8 = (bf16[512,256]{1,0:T(8,128)(2,1)S(1)}, bf16[512,256]{1,0:T(8,128)(2,1)S(1)}, u32[]{:S(2)}, u32[]{:S(2)}) collective-permute-start(bf16[512,256]{1,0:T(8,128)(2,1)S(1)} %pad_maximum_fusion.1.kv_ref), channel_id=1, source_target_pairs={{0,192},{16,208},{32,224},{48,240},{64,128},{80,144},{96,160},{112... | collective-permute-start | bytes 786440 | tf_op jit(solution)/shard_map/ppermute | solution.py:475
  23.5 12.5 %collective-permute-start.7 = (bf16[512,256]{1,0:T(8,128)(2,1)S(1)}, bf16[512,256]{1,0:T(8,128)(2,1)S(1)}, u32[]{:S(2)}, u32[]{:S(2)}) collective-permute-start(bf16[512,256]{1,0:T(8,128)(2,1)S(1)} %pad_maximum_fusion.1.kv_ref), channel_id=1, source_target_pairs={{0,128},{16,144},{32,160},{48,176},{64,192},{80,208},{96,224},{112... | collective-permute-start | bytes 786440 | tf_op jit(solution)/shard_map/ppermute | solution.py:475
  24.1 12.5 %collective-permute-start.6 = (bf16[512,256]{1,0:T(8,128)(2,1)S(1)}, bf16[512,256]{1,0:T(8,128)(2,1)S(1)}, u32[]{:S(2)}, u32[]{:S(2)}) collective-permute-start(bf16[512,256]{1,0:T(8,128)(2,1)S(1)} %pad_maximum_fusion.1.kv_ref), channel_id=1, source_target_pairs={{0,64},{16,80},{32,96},{48,112},{64,0},{80,16},{96,32},{112,48},{1... | collective-permute-start | bytes 786440 | tf_op jit(solution)/shard_map/ppermute | solution.py:475
  42.0 26.4 %collective-permute-start.11 = (bf16[512,256]{1,0:T(8,128)(2,1)S(1)}, bf16[512,256]{1,0:T(8,128)(2,1)S(1)}, u32[]{:S(2)}, u32[]{:S(2)}) collective-permute-start(bf16[512,256]{1,0:T(8,128)(2,1)S(1)} %get-tuple-element.45), channel_id=1, source_target_pairs={{0,128},{16,144},{32,160},{48,176},{64,192},{80,208},{96,224},{112... | collective-permute-start | bytes 786440 | tf_op jit(solution)/shard_map/ppermute | solution.py:475
  47.1 21.4 %collective-permute-start.12 = (bf16[512,256]{1,0:T(8,128)(2,1)S(1)}, bf16[512,256]{1,0:T(8,128)(2,1)S(1)}, u32[]{:S(2)}, u32[]{:S(2)}) collective-permute-start(bf16[512,256]{1,0:T(8,128)(2,1)S(1)} %get-tuple-element.46), channel_id=1, source_target_pairs={{0,192},{16,208},{32,224},{48,240},{64,128},{80,144},{96,160},{112... | collective-permute-start | bytes 786440 | tf_op jit(solution)/shard_map/ppermute | solution.py:475
  49.2 19.3 %collective-permute-start.10 = (bf16[512,256]{1,0:T(8,128)(2,1)S(1)}, bf16[512,256]{1,0:T(8,128)(2,1)S(1)}, u32[]{:S(2)}, u32[]{:S(2)}) collective-permute-start(bf16[512,256]{1,0:T(8,128)(2,1)S(1)} %get-tuple-element.40), channel_id=1, source_target_pairs={{0,64},{16,80},{32,96},{48,112},{64,0},{80,16},{96,32},{112,48},{1... | collective-permute-start | bytes 786440 | tf_op jit(solution)/shard_map/ppermute | solution.py:475
  64.3 23.0 %all-to-all-start.1 = ((bf16[16,160,128]{2,1,0:T(8,128)(2,1)}), bf16[16,160,128]{2,1,0:T(8,128)(2,1)S(1)}, u32[]{:S(2)}, u32[]{:S(2)}) async-start(bf16[16,160,128]{2,1,0:T(8,128)(2,1)} %experts.1), calls=%async_computation.1 | async-start | bytes 1310720 | tf_op jit(solution)/shard_map/all_to_all | solution.py:512
  68.4 18.9 %copy-start = (f32[160,128]{1,0:T(8,128)S(1)}, f32[160,128]{1,0:T(8,128)}, u32[]{:S(2)}) copy-start(f32[160,128]{1,0:T(8,128)} %get-tuple-element.47.weight_ref) | copy-start | bytes 245764
  68.6 6.6 %collective-permute-start.13 = (bf16[128,256]{1,0:T(8,128)(2,1)S(1)}, bf16[128,256]{1,0:T(8,128)(2,1)S(1)}, u32[]{:S(2)}, u32[]{:S(2)}) collective-permute-start(bf16[128,256]{1,0:T(8,128)(2,1)S(1)} %get-tuple-element.54), channel_id=1, source_target_pairs={{0,32},{16,48},{32,0},{48,16},{64,96},{80,112},{96,64},{112,80},{1... | collective-permute-start | bytes 196616 | tf_op jit(solution)/shard_map/ppermute | solution.py:475
  69.0 6.2 %collective-permute-start.15 = (bf16[128,256]{1,0:T(8,128)(2,1)S(1)}, bf16[128,256]{1,0:T(8,128)(2,1)S(1)}, u32[]{:S(2)}, u32[]{:S(2)}) collective-permute-start(bf16[128,256]{1,0:T(8,128)(2,1)S(1)} %get-tuple-element.55), channel_id=1, source_target_pairs={{0,48},{16,32},{32,16},{48,0},{64,112},{80,96},{96,80},{112,64},{1... | collective-permute-start | bytes 196616 | tf_op jit(solution)/shard_map/ppermute | solution.py:475
  70.2 5.1 %collective-permute-start.14 = (bf16[128,256]{1,0:T(8,128)(2,1)S(1)}, bf16[128,256]{1,0:T(8,128)(2,1)S(1)}, u32[]{:S(2)}, u32[]{:S(2)}) collective-permute-start(bf16[128,256]{1,0:T(8,128)(2,1)S(1)} %get-tuple-element.56), channel_id=1, source_target_pairs={{0,16},{16,0},{32,48},{48,32},{64,80},{80,64},{96,112},{112,96},{1... | collective-permute-start | bytes 196616 | tf_op jit(solution)/shard_map/ppermute | solution.py:475
  72.4 4.4 %collective-permute-start.9 = (bf16[2,512,128]{2,1,0:T(8,128)(2,1)S(1)}, bf16[2,512,128]{2,1,0:T(8,128)(2,1)S(1)}, u32[]{:S(2)}, u32[]{:S(2)}) collective-permute-start(bf16[2,512,128]{2,1,0:T(8,128)(2,1)S(1)} %get-tuple-element.42), channel_id=1, source_target_pairs={{0,16},{16,0},{32,48},{48,32},{64,80},{80,64},{96,112},{112,96},{1... | collective-permute-start | bytes 786440 | tf_op jit(solution)/shard_map/ppermute | solution.py:475

commit v3 on v2

--- a/solution.py
+++ b/solution.py
@@ -60,13 +60,13 @@
 
 
 def near_kernel(
-    scale, span_ref, q_own, q_got, d_own, d_got, stat_own, stat_got, kv_ref, dq_ref, sum_ref, stat_ref, keys_t, key_pos
+    scale, span_ref, q_own, q_got, d_own, d_got, stat_own, stat_got, kv_ref, dq_ref, sum_ref, stat_ref, keys, values, keys_t, key_pos
 ):
     me = lax.axis_index("ctx")
     chip, core = me // 2, me % 2
     span_of = span_finder(span_ref)
     width = q_own.shape[1]
-    count = kv_ref.shape[0]
+    count = kv_ref.shape[0] // 2
     half = count // 8
     repeat = width // half
 
@@ -86,7 +86,11 @@
     is_norm = lax.broadcasted_iota(jnp.int32, lanes.shape, 0) % 2 == 0
     stat_ref[...] = jnp.where(is_norm, lanes * (1.0 / math.log(2.0)), lanes)
 
-    keys_t[...] = kv_ref[:, :LANES].T
+    for device in range(4):
+        at = slice(device * 2 * half, (device + 1) * 2 * half)
+        keys[at, :] = kv_ref[device * 4 * half : device * 4 * half + 2 * half, :]
+        values[at, :] = kv_ref[device * 4 * half + 2 * half : (device + 1) * 4 * half, :]
+    keys_t[...] = keys[...].T
     for part in range(8):
         span = span_of(chip ^ (part // 4), part // 2 % 2, part % 2)
         at = slice(part * half, (part + 1) * half)
@@ -109,8 +113,8 @@
             d_ref[upper],
             stat_ref[line : line + 1, at],
             stat_ref[line + 1 : line + 2, at],
-            kv_ref[:, :LANES],
-            kv_ref[:, LANES:],
+            keys[...],
+            values[...],
             keys_t[...],
             visible,
         )
@@ -130,7 +134,7 @@
     span_of = span_finder(span_ref)
     slots = span_ref.shape[0]
     width = q_own.shape[1]
-    half = kv_refs[0].shape[0] // 8
+    half = kv_refs[0].shape[0] // 16
 
     for n in range(slots):
         before[n] = 0
@@ -153,9 +157,9 @@
     for block in range(kv_blocks):
         for part in range(8):
             at = place(block, part)
-            rows = kv_refs[block][part * half : (part + 1) * half, :]
-            keys[at, :] = rows[:, :LANES]
-            values[at, :] = rows[:, LANES:]
+            first = (part // 2 * 4 + part % 2) * half
+            keys[at, :] = kv_refs[block][first : first + half, :]
+            values[at, :] = kv_refs[block][first + 2 * half : first + 3 * half, :]
     for chunk in range(keys.shape[0] // CHUNK):
         at = slice(chunk * CHUNK, (chunk + 1) * CHUNK)
         keys_t[:, at] = keys[at, :].T
@@ -214,7 +218,7 @@
 
 
 def attention_near(span_order, q_own, q_got, d_own, d_got, stat_own, stat_got, kv, scale):
-    count = kv.shape[0]
+    count = kv.shape[0] // 2
     halves, width, size = q_own.shape
     assert count * 2 == LONG
     return pl.pallas_call(
@@ -226,7 +230,12 @@
         ),
         in_specs=[SMEM] + [VMEM] * 7,
         out_specs=(VMEM,) * 3,
-        scratch_shapes=[pltpu.VMEM((LANES, count), BF16), pltpu.VMEM((count, LANES), jnp.int32)],
+        scratch_shapes=[
+            pltpu.VMEM((count, LANES), BF16),
+            pltpu.VMEM((count, LANES), BF16),
+            pltpu.VMEM((LANES, count), BF16),
+            pltpu.VMEM((count, LANES), jnp.int32),
+        ],
         compiler_params=pltpu.CompilerParams(vmem_limit_bytes=16 * MIB),
         cost_estimate=pl.CostEstimate(
             flops=20 * halves * width * count * size,
@@ -239,7 +248,7 @@
 
 def attention_far(span_order, q_own, q_got, d_own, d_got, stats, dq_near, kv_list, scale):
     blocks = len(kv_list)
-    rows = kv_list[0].shape[0]
+    rows = kv_list[0].shape[0] // 2
     total = blocks * rows
     halves, width, size = q_own.shape
     assert total % LONG == LONG // 2
@@ -275,13 +284,14 @@
             chunk_ref[expert, at : at + SLOT, :] = tiles[block, expert * SLOT : (expert + 1) * SLOT, :]
 
 
-def dispatch_kernel(ids_ref, keep_ref, weight_ref, x_hbm, g_hbm, send_ref, combine_ref, x_ref, g_ref, tiles, chunks, sems):
-    loads = [
-        pltpu.make_async_copy(source, target, sems.at[i])
-        for i, (source, target) in enumerate(((x_hbm, x_ref), (g_hbm, g_ref)))
-    ]
+def dispatch_kernel(*refs):
+    sources, (send_ref, combine_ref), targets, (tiles, chunks, sems) = refs[:5], refs[5:7], refs[7:12], refs[12:]
+    ids_ref, keep_ref, weight_ref, x_ref, g_ref = targets
+    loads = [pltpu.make_async_copy(*pair, sems.at[i]) for i, pair in enumerate(zip(sources, targets))]
     for load in loads:
         load.start()
+    for load in loads[:3]:
+        load.wait()
     top, rows = ids_ref.shape
     experts = send_ref.shape[0]
     blocks = x_ref.shape[1] // LANES
@@ -305,7 +315,7 @@
     chosen = jnp.where(rank == slot_of.astype(F32), hit, 0.0)
     combine_ref[...] = chosen * weight
     pick = chosen.astype(BF16)
-    for load, source, first in ((loads[0], x_ref, 0), (loads[1], g_ref, blocks * SLOT)):
+    for load, source, first in ((loads[3], x_ref, 0), (loads[4], g_ref, blocks * SLOT)):
         load.wait()
         for pair in range(blocks // 2):
             both = dot(pick, source[:, pair * 2 * LANES : (pair + 1) * 2 * LANES])
@@ -325,14 +335,17 @@
             jax.ShapeDtypeStruct((experts, 2 * blocks * SLOT, LANES), BF16),
             jax.ShapeDtypeStruct((slots, rows), F32),
         ),
-        in_specs=[VMEM] * 3 + [ANY] * 2,
+        in_specs=[ANY] * 5,
         out_specs=(VMEM, VMEM),
         scratch_shapes=[
+            pltpu.VMEM(ids.T.shape, ids.dtype),
+            pltpu.VMEM(ids.T.shape, keep.dtype),
+            pltpu.VMEM(ids.T.shape, weight.dtype),
             pltpu.VMEM(x.shape, BF16),
             pltpu.VMEM(g.shape, BF16),
             pltpu.VMEM((blocks, slots, LANES), F32),
             pltpu.VMEM((experts, 2 * blocks * SLOT, LANES), F32),
-            pltpu.SemaphoreType.DMA((2,)),
+            pltpu.SemaphoreType.DMA((5,)),
         ],
         compiler_params=pltpu.CompilerParams(vmem_limit_bytes=60 * MIB),
         name="dispatch",
@@ -349,13 +362,15 @@
     hidden = weights[0].shape[1]
     tile = 256
     loads = []
-    for step in range(hidden // tile):
-        part = slice(step * tile, (step + 1) * tile)
+    edges = [0, tile // 2, hidden // 2, hidden]
+    parts = [slice(low, high) for low, high in zip(edges, edges[1:])]
+    for step, part in enumerate(parts):
         for i in range(3):
             at = (slice(None), part) if i < 2 else (part, slice(None))
             load = pltpu.make_async_copy(weights_hbm[i].at[(0,) + at], weights[i].at[at], sems.at[3 * step + i])
-            load.start()
             loads.append(load)
+    for load in loads[:3]:
+        load.start()
     chunks[...] = in_ref[...].astype(F32)
     for rows_ref, first in ((x_rows, 0), (g_rows, blocks * SLOT)):
         for block in range(blocks):
@@ -363,22 +378,29 @@
                 at = first + block * SLOT
                 tiles[block, source * SLOT : (source + 1) * SLOT, :] = chunks[source, at : at + SLOT, :]
             rows_ref[:, block * LANES : (block + 1) * LANES] = tiles[block].astype(BF16)
-    total = None
-    for step in range(hidden // tile):
+    for load in loads[3:]:
+        load.start()
+
+    def back(part, gate_grad, up_grad, fresh):
+        term = dot_rows(gate_grad, weights[0][:, part]) + dot_rows(up_grad, weights[1][:, part])
+        for block in range(blocks):
+            piece = term[:, block * LANES : (block + 1) * LANES]
+            tiles[block] = piece if fresh else tiles[block] + piece
+
+    waiting = None
+    for step, part in enumerate(parts):
         for i in range(3):
             loads[3 * step + i].wait()
-        part = slice(step * tile, (step + 1) * tile)
-        gate_w, up_w = weights[0][:, part], weights[1][:, part]
-        gate_pre = dot(x_rows[...], gate_w)
-        up_pre = dot(x_rows[...], up_w)
+        gate_pre = dot(x_rows[...], weights[0][:, part])
+        up_pre = dot(x_rows[...], weights[1][:, part])
         hidden_grad = dot_rows(g_rows[...], weights[2][part, :])
+        if waiting is not None:
+            back(*waiting, step == 1)
         sig = jax.nn.sigmoid(gate_pre)
         gate_grad = (hidden_grad * up_pre * sig * (1.0 + gate_pre * (1.0 - sig))).astype(BF16)
         up_grad = (hidden_grad * gate_pre * sig).astype(BF16)
-        term = dot_rows(gate_grad, gate_w) + dot_rows(up_grad, up_w)
-        for block in range(blocks):
-            piece = term[:, block * LANES : (block + 1) * LANES]
-            tiles[block] = piece if step == 0 else tiles[block] + piece
+        waiting = (part, gate_grad, up_grad)
+    back(*waiting, False)
     slots_to_chunks(tiles, sources, blocks, chunks, 0)
     out_ref[...] = chunks[:, : blocks * SLOT, :].astype(BF16)
 
@@ -474,7 +496,7 @@
     chips = members // 2
     trade = lambda array, k: lax.ppermute(array, "ctx", [(i, i ^ k) for i in range(members)])
 
-    kv = jnp.concatenate([key_tensor, value_tensor], axis=2)
+    kv = jnp.stack([key_tensor, value_tensor]).reshape(2 * rows, 2, size)
     kv_own = jnp.where(first, kv[:, 0], kv[:, 1])
     kv_away = jnp.where(first, kv[:, 1], kv[:, 0])
     kv_own, kv_away, expert_ids = lax.optimization_barrier((kv_own, kv_away, expert_ids))
@@ -482,7 +504,8 @@
     kv_near, kv_cross = trade(kv_own, 2), trade(kv_away, 3)
     send, weight = dispatch(expert_ids, keep_mask, route_weight, moe_input, moe_grad, experts)
     ordered = lambda mine, other: [jnp.where(first, mine, other), jnp.where(first, other, mine)]
-    kv_pair = jnp.concatenate(ordered(kv_own, kv_got) + ordered(kv_near, kv_cross), axis=0)
+    pieces = ordered(kv_own, kv_got) + ordered(kv_near, kv_cross)
+    kv_pair = jnp.concatenate(pieces, axis=0)
     send, kv_pair = lax.optimization_barrier((send, kv_pair))
     received = lax.all_to_all(send, "exp", split_axis=0, concat_axis=0, tiled=True)
     kv_list = [trade(kv_pair, 4 * k) for k in range(1, chips // 2)]

time: 90.6 us -> 87.8 us (0.969); the launches traced: 88.8 us -> 87.3 us
  starting transfers between devices: 33 us -> 30.7 us
  local copies, waits for them, and re-layouts: 3.23 us -> 1.45 us
  other arithmetic: 1.31 us -> 2.43 us
    pallas_call x1, Pallas kernels: 5.42 us -> 8.09 us  [attention_far(): pl.pallas_call(functools.partial(far_kernel, scale, blocks), out_shape=(j...]
    ppermute x16, starting transfers between devices: 20.1 us -> 17.6 us  [on_device(): lax.ppermute(array, 'ctx', [(i, i ^ k) for i in range(members)])]
    pallas_call x1, Pallas kernels: 10.6 us -> 9.4 us  [mlp(): pl.pallas_call(mlp_kernel, out_shape=jax.ShapeDtypeStruct((sources, block...]
    another operation x0 -> x1, other arithmetic: none -> 1.12 us  [on_device(): kv = jnp.stack([key_tensor, value_tensor]).reshape(2 * rows, 2, size)]
    ppermute x16, waiting for transfers between devices: 12.1 us -> 13.2 us  [on_device(): lax.ppermute(array, 'ctx', [(i, i ^ k) for i in range(members)])]
    unnamed x15 -> x14, local copies, waits for them, and re-layouts: 2.36 us -> 1.43 us
  transfers between devices with their start and end apart: 18 -> 18, of which waited for: 6 -> 6; matrix products, arithmetic and copies ran while one was open for 3% -> 3% of each run, Pallas kernels for 26% -> 28%
where the time goes in v3:
time: 87.8 us; the launch traced here: 87.3 us
  starting transfers between devices  30.7 us (35%)
  waiting for transfers between devices  26.1 us (30%)
  Pallas kernels  25.6 us (29%)
  other arithmetic  2.43 us (3%)
  local copies, waits for them, and re-layouts  1.45 us (2%)
  between operations  0.92 us (1%)
    ppermute x16, starting transfers between devices, on_device(): lax.ppermute(array, 'ctx', [(i, i ^ k) for i in range(members)])  17.6 us
    ppermute x16, waiting for transfers between devices, on_device(): lax.ppermute(array, 'ctx', [(i, i ^ k) for i in range(members)])  13.2 us
    all_to_all x1, waiting for transfers between devices, on_device(): lax.all_to_all(slot_grad, 'exp', split_axis=0, concat_axis=0, tiled=True)  9.5 us
    pallas_call x1, Pallas kernels, mlp(): pl.pallas_call(mlp_kernel, out_shape=jax.ShapeDtypeStruct((sources, block...  9.4 us
    all_to_all x1, starting transfers between devices, on_device(): lax.all_to_all(send, 'exp', split_axis=0, concat_axis=0, tiled=True)  8.52 us
    pallas_call x1, Pallas kernels, attention_far(): pl.pallas_call(functools.partial(far_kernel, scale, blocks), out_shape=(j...  8.09 us
    all_to_all x1, starting transfers between devices, on_device(): lax.all_to_all(slot_grad, 'exp', split_axis=0, concat_axis=0, tiled=True)  4.62 us
    all_to_all x1, waiting for transfers between devices, on_device(): lax.all_to_all(send, 'exp', split_axis=0, concat_axis=0, tiled=True)  3.46 us
  transfers between devices with their start and end apart: 18, of which 6 were waited for; matrix products, arithmetic and copies ran while one was open for 3% of the time, Pallas kernels for 28%

profile of v3, /device:TPU:4, one launch (start us, length us, event | category | flops | bytes accessed | tf_op | source)
XLA Modules:
  0.0 87.3 jit_solution(14730778122784618434)
XLA Ops:
  0.6 0.0 copy-start.2
  0.6 1.1 %pad_maximum_fusion.2 = bf16[2,128,2,128]{3,2,1,0:T(2,128)(2,1)S(1)} fusion(bf16[1,128,2,128]{3,2,1,0:T(2,128)(2,1)} %bitcast.41, bf16[1,128,2,128]{3,2,1,0:T(2,128)(2,1)} %bitcast.42), kind=kLoop, calls=%fused_computation.9 | loop fusion | flops 65536 | bytes 262144 | tf_op jit(solution)/shard_map/stack | solution.py:499
  1.8 0.0 copy-start.3
  1.8 0.1 collective-permute-start.4
  1.9 2.4 %collective-permute-start.5 = (bf16[256,128]{1,0:T(8,128)(2,1)S(1)}, bf16[256,128]{1,0:T(8,128)(2,1)S(1)}, u32[]{:S(2)}, u32[]{:S(2)}) collective-permute-start(bf16[256,128]{1,0:T(8,128)(2,1)S(1)} %get-tuple-element.33), channel_id=1, source_target_pairs={{0,48},{16,32},{32,16},{48,0},{64,112},{80,96},{96,80},{112,64},{1... | collective-permute-start | bytes 196616 | tf_op jit(solution)/shard_map/ppermute | solution.py:497
  4.3 1.3 %collective-permute-start = (bf16[256,128]{1,0:T(8,128)(2,1)S(1)}, bf16[256,128]{1,0:T(8,128)(2,1)S(1)}, u32[]{:S(2)}, u32[]{:S(2)}) collective-permute-start(bf16[256,128]{1,0:T(8,128)(2,1)S(1)} %get-tuple-element.26), channel_id=1, source_target_pairs={{0,32},{16,48},{32,0},{48,16},{64,96},{80,112},{96,64},{112,80},{1... | collective-permute-start | bytes 196616 | tf_op jit(solution)/shard_map/ppermute | solution.py:497
  5.6 3.2 %dispatch.1 = (bf16[16,320,128]{2,1,0:T(8,128)(2,1)}, f32[160,128]{1,0:T(8,128)}) custom-call(s32[8,128]{1,0:T(8,128)} %bitcast.45, s32[8,128]{1,0:T(8,128)} %bitcast.46, f32[8,128]{1,0:T(8,128)} %bitcast.47, bf16[128,2048]{1,0:T(8,128)(2,1)} %refs_3_.1, bf16[128,2048]{1,0:T(8,128)(2,1)} %refs_4_.1), custom_call_target="tpu_custom_call" | custom-call | tf_op jit(solution)/shard_map/dispatch/pallas_call | solution.py:332
  8.8 0.0 copy-start.4
  8.8 0.0 copy-start.5
  8.8 0.0 copy-start.1
  8.8 0.0 collective-permute-done.4
  8.8 1.2 %collective-permute-done = bf16[256,128]{1,0:T(8,128)(2,1)S(1)} collective-permute-done((bf16[256,128]{1,0:T(8,128)(2,1)S(1)}, bf16[256,128]{1,0:T(8,128)(2,1)S(1)}, u32[]{:S(2)}, u32[]{:S(2)}) %collective-permute-start) | collective-permute-done | bytes 65568 | tf_op jit(solution)/shard_map/ppermute | solution.py:497
  10.1 0.0 collective-permute-done.5
  10.1 8.5 %all-to-all-start = ((bf16[16,320,128]{2,1,0:T(8,128)(2,1)}), bf16[16,320,128]{2,1,0:T(8,128)(2,1)}, u32[]{:S(2)}, u32[]{:S(2)}) async-start(bf16[16,320,128]{2,1,0:T(8,128)(2,1)} %get-tuple-element.39), calls=%async_computation | async-start | bytes 2621440 | tf_op jit(solution)/shard_map/all_to_all | solution.py:510
  18.6 0.0 copy-done.2
  18.7 0.1 collective-permute-start.1
  18.8 0.0 copy-done.3
  18.9 0.6 collective-permute-start.2
  19.4 0.0 copy-done.4
  19.4 0.0 copy-done.5
  19.4 0.1 collective-permute-start.3
  19.6 3.1 %collective-permute-start.8 = (bf16[1024,128]{1,0:T(8,128)(2,1)S(1)}, bf16[1024,128]{1,0:T(8,128)(2,1)S(1)}, u32[]{:S(2)}, u32[]{:S(2)}) collective-permute-start(bf16[1024,128]{1,0:T(8,128)(2,1)S(1)} %pad_maximum_fusion.1.kv_ref), channel_id=1, source_target_pairs={{0,192},{16,208},{32,224},{48,240},{64,128},{80,144},{96,160},{112... | collective-permute-start | bytes 786440 | tf_op jit(solution)/shard_map/ppermute | solution.py:497
  22.6 0.6 collective-permute-start.7
  23.3 0.0 collective-permute-done.3
  23.3 0.5 collective-permute-start.6
  23.7 0.0 collective-permute-done.1
  23.7 0.0 collective-permute-done.2
  23.7 0.0 copy-done.1
  23.7 3.4 %attention_near.1 = (f32[4,128,512]{2,1,0:T(8,128)S(1)}, f32[512,256]{1,0:T(8,128)S(1)}, f32[4,1024]{1,0:T(4,128)S(1)}) custom-call(s32[32]{0:T(128)S(1)} %copy-done.1, bf16[2,512,128]{2,1,0:T(8,128)(2,1)S(1)} %bitcast.29, bf16[2,512,128]{2,1,0:T(8,128)(2,1)S(1)} %bitcast.33, bf16[2,512,128]{2,1,0:T(8,128)(2,1)S(1)} %bitcast.31, ...), custom_call_target="tpu_custom_call" | custom-call | flops 1342177280 | bytes 3145728 | tf_op jit(solution)/shard_map/attention_near/pallas_call | solution.py:224
  27.2 8.0 %collective-permute-done.8.rest_2_ = bf16[1024,128]{1,0:T(8,128)(2,1)S(1)} collective-permute-done((bf16[1024,128]{1,0:T(8,128)(2,1)S(1)}, bf16[1024,128]{1,0:T(8,128)(2,1)S(1)}, u32[]{:S(2)}, u32[]{:S(2)}) %collective-permute-start.8) | collective-permute-done | bytes 262176 | tf_op jit(solution)/shard_map/ppermute | solution.py:497
  35.1 0.0 collective-permute-done.7.rest_1_
  35.1 0.6 collective-permute-done.6.rest_0_
  35.8 8.1 %attention_far.1 = (bf16[2,512,128]{2,1,0:T(8,128)(2,1)S(1)}, bf16[2,512,128]{2,1,0:T(8,128)(2,1)S(1)}, bf16[512,256]{1,0:T(8,128)(2,1)S(1)}, bf16[512,256]{1,0:T(8,128)(2,1)S(1)}, bf16[512,256]{1,0:T(8,128)(2,1)S(1)}) custom-call(s32[32]{0:T(128)S(1)} %copy-done.1, bf16[2,512,128]{2,1,0:T(8,128)(2,1)S(1)} %bitcast.30, bf16[2,512,128]{2,1,0:T(8,128)(2,1)S(1)} %bitcast.34, ...), custom_call_target="tpu_custom_call" | custom-call | flops 4026531840 | bytes 6291456 | tf_op jit(solution)/shard_map/attention_far/pallas_call | solution.py:256
  43.9 2.1 %collective-permute-start.11 = (bf16[512,256]{1,0:T(8,128)(2,1)S(1)}, bf16[512,256]{1,0:T(8,128)(2,1)S(1)}, u32[]{:S(2)}, u32[]{:S(2)}) collective-permute-start(bf16[512,256]{1,0:T(8,128)(2,1)S(1)} %get-tuple-element.45), channel_id=1, source_target_pairs={{0,128},{16,144},{32,160},{48,176},{64,192},{80,208},{96,224},{112... | collective-permute-start | bytes 786440 | tf_op jit(solution)/shard_map/ppermute | solution.py:497
  45.9 3.1 %collective-permute-start.12 = (bf16[512,256]{1,0:T(8,128)(2,1)S(1)}, bf16[512,256]{1,0:T(8,128)(2,1)S(1)}, u32[]{:S(2)}, u32[]{:S(2)}) collective-permute-start(bf16[512,256]{1,0:T(8,128)(2,1)S(1)} %get-tuple-element.46), channel_id=1, source_target_pairs={{0,192},{16,208},{32,224},{48,240},{64,128},{80,144},{96,160},{112... | collective-permute-start | bytes 786440 | tf_op jit(solution)/shard_map/ppermute | solution.py:497
  49.1 0.0 collective-permute-start.10
  49.1 3.5 %all-to-all-done.in_ref = bf16[16,320,128]{2,1,0:T(8,128)(2,1)} async-done(((bf16[16,320,128]{2,1,0:T(8,128)(2,1)}), bf16[16,320,128]{2,1,0:T(8,128)(2,1)}, u32[]{:S(2)}, u32[]{:S(2)}) %all-to-all-start) | async-done | bytes 1310752 | tf_op jit(solution)/shard_map/all_to_all | solution.py:510
  52.5 9.4 %experts.1 = bf16[16,160,128]{2,1,0:T(8,128)(2,1)} custom-call(bf16[16,320,128]{2,1,0:T(8,128)(2,1)} %all-to-all-done.in_ref, bf16[1,2048,768]{2,1,0:T(8,128)(2,1)} %rest_0_.1, bf16[1,2048,768]{2,1,0:T(8,128)(2,1)} %rest_1_.1, bf16[1,768,2048]{2,1,0:T(8,128)(2,1)} %rest_2_.1), custom_call_target="tpu_custom_call" | custom-call | flops 2516582400 | bytes 11534336 | tf_op jit(solution)/shard_map/experts/pallas_call | solution.py:413
  61.9 4.6 %all-to-all-start.1 = ((bf16[16,160,128]{2,1,0:T(8,128)(2,1)}), bf16[16,160,128]{2,1,0:T(8,128)(2,1)S(1)}, u32[]{:S(2)}, u32[]{:S(2)}) async-start(bf16[16,160,128]{2,1,0:T(8,128)(2,1)} %experts.1), calls=%async_computation.1 | async-start | bytes 1310720 | tf_op jit(solution)/shard_map/all_to_all | solution.py:535
  66.6 0.0 copy-start
  66.6 0.0 collective-permute-done.11
  66.6 0.0 collective-permute-done.12
  66.6 0.0 collective-permute-done.10
  66.6 0.1 convert_add_fusion
  66.8 0.6 collective-permute-start.13
  67.4 0.9 %collective-permute-start.15 = (bf16[128,256]{1,0:T(8,128)(2,1)S(1)}, bf16[128,256]{1,0:T(8,128)(2,1)S(1)}, u32[]{:S(2)}, u32[]{:S(2)}) collective-permute-start(bf16[128,256]{1,0:T(8,128)(2,1)S(1)} %get-tuple-element.55), channel_id=1, source_target_pairs={{0,48},{16,32},{32,16},{48,0},{64,112},{80,96},{96,80},{112,64},{1... | collective-permute-start | bytes 196616 | tf_op jit(solution)/shard_map/ppermute | solution.py:497
  68.3 2.2 %collective-permute-start.14 = (bf16[128,256]{1,0:T(8,128)(2,1)S(1)}, bf16[128,256]{1,0:T(8,128)(2,1)S(1)}, u32[]{:S(2)}, u32[]{:S(2)}) collective-permute-start(bf16[128,256]{1,0:T(8,128)(2,1)S(1)} %get-tuple-element.56), channel_id=1, source_target_pairs={{0,16},{16,0},{32,48},{48,32},{64,80},{80,64},{96,112},{112,96},{1... | collective-permute-start | bytes 196616 | tf_op jit(solution)/shard_map/ppermute | solution.py:497
  70.5 0.0 collective-permute-start.9
  70.5 3.3 %collective-permute-done.13 = bf16[128,256]{1,0:T(8,128)(2,1)S(1)} collective-permute-done((bf16[128,256]{1,0:T(8,128)(2,1)S(1)}, bf16[128,256]{1,0:T(8,128)(2,1)S(1)}, u32[]{:S(2)}, u32[]{:S(2)}) %collective-permute-start.13) | collective-permute-done | bytes 65568 | tf_op jit(solution)/shard_map/ppermute | solution.py:497
  73.8 0.0 collective-permute-done.15
  73.8 0.0 collective-permute-done.14
  73.9 0.7 copy.21
  74.6 0.7 copy.20
  75.3 0.0 collective-permute-done.9
  75.4 0.9 %pad_maximum_fusion = bf16[128,16,128]{2,1,0:T(8,128)(2,1)} fusion(bf16[128,8,128]{2,1,0:T(8,128)(2,1)S(1)} %bitcast.39, bf16[128,8,128]{2,1,0:T(8,128)(2,1)S(1)} %bitcast.38), kind=kLoop, calls=%fused_computation | loop fusion | flops 1048576 | bytes 1048576 | tf_op jit(solution)/shard_map/concatenate | solution.py:548
  76.2 9.5 %all-to-all-done.1.back_ref = bf16[16,160,128]{2,1,0:T(8,128)(2,1)S(1)} async-done(((bf16[16,160,128]{2,1,0:T(8,128)(2,1)}), bf16[16,160,128]{2,1,0:T(8,128)(2,1)S(1)}, u32[]{:S(2)}, u32[]{:S(2)}) %all-to-all-start.1) | async-done | bytes 655392 | tf_op jit(solution)/shard_map/all_to_all | solution.py:535
  85.7 0.0 copy-done
  85.7 1.5 %combine.1 = bf16[128,2048]{1,0:T(8,128)(2,1)} custom-call(f32[160,128]{1,0:T(8,128)S(1)} %copy-done, bf16[16,160,128]{2,1,0:T(8,128)(2,1)S(1)} %all-to-all-done.1.back_ref), custom_call_target="tpu_custom_call" | custom-call | tf_op jit(solution)/shard_map/combine/pallas_call | solution.py:459
  (13 shorter events, 0.3 us)
Async XLA Ops:
  0.6 18.0 %copy-start.2 = (bf16[128,16,128]{2,1,0:T(8,128)(2,1)S(1)}, bf16[128,16,128]{2,1,0:T(8,128)(2,1)}, u32[]{:S(2)}) copy-start(bf16[128,16,128]{2,1,0:T(8,128)(2,1)} %param.15) | copy-start | bytes 1572868
  1.8 17.0 %copy-start.3 = (bf16[128,16,128]{2,1,0:T(8,128)(2,1)S(1)}, bf16[128,16,128]{2,1,0:T(8,128)(2,1)}, u32[]{:S(2)}) copy-start(bf16[128,16,128]{2,1,0:T(8,128)(2,1)} %param.18) | copy-start | bytes 1572868
  1.8 7.0 %collective-permute-start.4 = (bf16[256,128]{1,0:T(8,128)(2,1)S(1)}, bf16[256,128]{1,0:T(8,128)(2,1)S(1)}, u32[]{:S(2)}, u32[]{:S(2)}) collective-permute-start(bf16[256,128]{1,0:T(8,128)(2,1)S(1)} %get-tuple-element.33), channel_id=1, source_target_pairs={{0,16},{16,0},{32,48},{48,32},{64,80},{80,64},{96,112},{112,96},{1... | collective-permute-start | bytes 196616 | tf_op jit(solution)/shard_map/ppermute | solution.py:497
  1.9 8.1 %collective-permute-start.5 = (bf16[256,128]{1,0:T(8,128)(2,1)S(1)}, bf16[256,128]{1,0:T(8,128)(2,1)S(1)}, u32[]{:S(2)}, u32[]{:S(2)}) collective-permute-start(bf16[256,128]{1,0:T(8,128)(2,1)S(1)} %get-tuple-element.33), channel_id=1, source_target_pairs={{0,48},{16,32},{32,16},{48,0},{64,112},{80,96},{96,80},{112,64},{1... | collective-permute-start | bytes 196616 | tf_op jit(solution)/shard_map/ppermute | solution.py:497
  4.3 5.8 %collective-permute-start = (bf16[256,128]{1,0:T(8,128)(2,1)S(1)}, bf16[256,128]{1,0:T(8,128)(2,1)S(1)}, u32[]{:S(2)}, u32[]{:S(2)}) collective-permute-start(bf16[256,128]{1,0:T(8,128)(2,1)S(1)} %get-tuple-element.26), channel_id=1, source_target_pairs={{0,32},{16,48},{32,0},{48,16},{64,96},{80,112},{96,64},{112,80},{1... | collective-permute-start | bytes 196616 | tf_op jit(solution)/shard_map/ppermute | solution.py:497
  8.8 10.7 %copy-start.4 = (f32[128,16]{0,1:T(8,128)S(1)}, f32[128,16]{0,1:T(8,128)}, u32[]{:S(2)}) copy-start(f32[128,16]{0,1:T(8,128)} %param.20) | copy-start | bytes 24580
  8.8 10.7 %copy-start.5 = (f32[128,16]{0,1:T(8,128)S(1)}, f32[128,16]{0,1:T(8,128)}, u32[]{:S(2)}) copy-start(f32[128,16]{0,1:T(8,128)} %param.19) | copy-start | bytes 24580
  8.8 15.0 %copy-start.1 = (s32[32]{0:T(128)S(1)}, s32[32]{0:T(128)}, u32[]{:S(2)}) copy-start(s32[32]{0:T(128)} %span_ref.3) | copy-start | bytes 388
  10.1 42.4 %all-to-all-start = ((bf16[16,320,128]{2,1,0:T(8,128)(2,1)}), bf16[16,320,128]{2,1,0:T(8,128)(2,1)}, u32[]{:S(2)}, u32[]{:S(2)}) async-start(bf16[16,320,128]{2,1,0:T(8,128)(2,1)} %get-tuple-element.39), calls=%async_computation | async-start | bytes 2621440 | tf_op jit(solution)/shard_map/all_to_all | solution.py:510
  18.7 5.0 %collective-permute-start.1 = (bf16[128,8,128]{2,1,0:T(8,128)(2,1)S(1)}, bf16[128,8,128]{2,1,0:T(8,128)(2,1)S(1)}, u32[]{:S(2)}, u32[]{:S(2)}) collective-permute-start(bf16[128,8,128]{2,1,0:T(8,128)(2,1)S(1)} %get-tuple-element.61), channel_id=1, source_target_pairs={{0,16},{16,0},{32,48},{48,32},{64,80},{80,64},{96,112},{112,96},{1... | collective-permute-start | bytes 786440 | tf_op jit(solution)/shard_map/ppermute | solution.py:497
  18.9 4.9 %collective-permute-start.2 = (bf16[128,8,128]{2,1,0:T(8,128)(2,1)S(1)}, bf16[128,8,128]{2,1,0:T(8,128)(2,1)S(1)}, u32[]{:S(2)}, u32[]{:S(2)}) collective-permute-start(bf16[128,8,128]{2,1,0:T(8,128)(2,1)S(1)} %get-tuple-element.59), channel_id=1, source_target_pairs={{0,16},{16,0},{32,48},{48,32},{64,80},{80,64},{96,112},{112,96},{1... | collective-permute-start | bytes 786440 | tf_op jit(solution)/shard_map/ppermute | solution.py:497
  19.4 3.8 %collective-permute-start.3 = (f32[2,8,128]{2,1,0:T(8,128)S(1)}, f32[2,8,128]{2,1,0:T(8,128)S(1)}, u32[]{:S(2)}, u32[]{:S(2)}) collective-permute-start(f32[2,8,128]{2,1,0:T(8,128)S(1)} %get-tuple-element.71), channel_id=1, source_target_pairs={{0,16},{16,0},{32,48},{48,32},{64,80},{80,64},{96,112},{112,96},{1... | collective-permute-start | bytes 24584 | tf_op jit(solution)/shard_map/ppermute | solution.py:497
  19.6 15.6 %collective-permute-start.8 = (bf16[1024,128]{1,0:T(8,128)(2,1)S(1)}, bf16[1024,128]{1,0:T(8,128)(2,1)S(1)}, u32[]{:S(2)}, u32[]{:S(2)}) collective-permute-start(bf16[1024,128]{1,0:T(8,128)(2,1)S(1)} %pad_maximum_fusion.1.kv_ref), channel_id=1, source_target_pairs={{0,192},{16,208},{32,224},{48,240},{64,128},{80,144},{96,160},{112... | collective-permute-start | bytes 786440 | tf_op jit(solution)/shard_map/ppermute | solution.py:497
  22.6 12.5 %collective-permute-start.7 = (bf16[1024,128]{1,0:T(8,128)(2,1)S(1)}, bf16[1024,128]{1,0:T(8,128)(2,1)S(1)}, u32[]{:S(2)}, u32[]{:S(2)}) collective-permute-start(bf16[1024,128]{1,0:T(8,128)(2,1)S(1)} %pad_maximum_fusion.1.kv_ref), channel_id=1, source_target_pairs={{0,128},{16,144},{32,160},{48,176},{64,192},{80,208},{96,224},{112... | collective-permute-start | bytes 786440 | tf_op jit(solution)/shard_map/ppermute | solution.py:497
  23.3 12.5 %collective-permute-start.6 = (bf16[1024,128]{1,0:T(8,128)(2,1)S(1)}, bf16[1024,128]{1,0:T(8,128)(2,1)S(1)}, u32[]{:S(2)}, u32[]{:S(2)}) collective-permute-start(bf16[1024,128]{1,0:T(8,128)(2,1)S(1)} %pad_maximum_fusion.1.kv_ref), channel_id=1, source_target_pairs={{0,64},{16,80},{32,96},{48,112},{64,0},{80,16},{96,32},{112,48},{1... | collective-permute-start | bytes 786440 | tf_op jit(solution)/shard_map/ppermute | solution.py:497
  43.9 22.7 %collective-permute-start.11 = (bf16[512,256]{1,0:T(8,128)(2,1)S(1)}, bf16[512,256]{1,0:T(8,128)(2,1)S(1)}, u32[]{:S(2)}, u32[]{:S(2)}) collective-permute-start(bf16[512,256]{1,0:T(8,128)(2,1)S(1)} %get-tuple-element.45), channel_id=1, source_target_pairs={{0,128},{16,144},{32,160},{48,176},{64,192},{80,208},{96,224},{112... | collective-permute-start | bytes 786440 | tf_op jit(solution)/shard_map/ppermute | solution.py:497
  45.9 20.6 %collective-permute-start.12 = (bf16[512,256]{1,0:T(8,128)(2,1)S(1)}, bf16[512,256]{1,0:T(8,128)(2,1)S(1)}, u32[]{:S(2)}, u32[]{:S(2)}) collective-permute-start(bf16[512,256]{1,0:T(8,128)(2,1)S(1)} %get-tuple-element.46), channel_id=1, source_target_pairs={{0,192},{16,208},{32,224},{48,240},{64,128},{80,144},{96,160},{112... | collective-permute-start | bytes 786440 | tf_op jit(solution)/shard_map/ppermute | solution.py:497
  49.1 17.5 %collective-permute-start.10 = (bf16[512,256]{1,0:T(8,128)(2,1)S(1)}, bf16[512,256]{1,0:T(8,128)(2,1)S(1)}, u32[]{:S(2)}, u32[]{:S(2)}) collective-permute-start(bf16[512,256]{1,0:T(8,128)(2,1)S(1)} %get-tuple-element.40), channel_id=1, source_target_pairs={{0,64},{16,80},{32,96},{48,112},{64,0},{80,16},{96,32},{112,48},{1... | collective-permute-start | bytes 786440 | tf_op jit(solution)/shard_map/ppermute | solution.py:497
  61.9 23.8 %all-to-all-start.1 = ((bf16[16,160,128]{2,1,0:T(8,128)(2,1)}), bf16[16,160,128]{2,1,0:T(8,128)(2,1)S(1)}, u32[]{:S(2)}, u32[]{:S(2)}) async-start(bf16[16,160,128]{2,1,0:T(8,128)(2,1)} %experts.1), calls=%async_computation.1 | async-start | bytes 1310720 | tf_op jit(solution)/shard_map/all_to_all | solution.py:535
  66.6 19.2 %copy-start = (f32[160,128]{1,0:T(8,128)S(1)}, f32[160,128]{1,0:T(8,128)}, u32[]{:S(2)}) copy-start(f32[160,128]{1,0:T(8,128)} %get-tuple-element.47.weight_ref) | copy-start | bytes 245764
  66.8 7.0 %collective-permute-start.13 = (bf16[128,256]{1,0:T(8,128)(2,1)S(1)}, bf16[128,256]{1,0:T(8,128)(2,1)S(1)}, u32[]{:S(2)}, u32[]{:S(2)}) collective-permute-start(bf16[128,256]{1,0:T(8,128)(2,1)S(1)} %get-tuple-element.54), channel_id=1, source_target_pairs={{0,32},{16,48},{32,0},{48,16},{64,96},{80,112},{96,64},{112,80},{1... | collective-permute-start | bytes 196616 | tf_op jit(solution)/shard_map/ppermute | solution.py:497
  67.4 6.4 %collective-permute-start.15 = (bf16[128,256]{1,0:T(8,128)(2,1)S(1)}, bf16[128,256]{1,0:T(8,128)(2,1)S(1)}, u32[]{:S(2)}, u32[]{:S(2)}) collective-permute-start(bf16[128,256]{1,0:T(8,128)(2,1)S(1)} %get-tuple-element.55), channel_id=1, source_target_pairs={{0,48},{16,32},{32,16},{48,0},{64,112},{80,96},{96,80},{112,64},{1... | collective-permute-start | bytes 196616 | tf_op jit(solution)/shard_map/ppermute | solution.py:497
  68.3 5.5 %collective-permute-start.14 = (bf16[128,256]{1,0:T(8,128)(2,1)S(1)}, bf16[128,256]{1,0:T(8,128)(2,1)S(1)}, u32[]{:S(2)}, u32[]{:S(2)}) collective-permute-start(bf16[128,256]{1,0:T(8,128)(2,1)S(1)} %get-tuple-element.56), channel_id=1, source_target_pairs={{0,16},{16,0},{32,48},{48,32},{64,80},{80,64},{96,112},{112,96},{1... | collective-permute-start | bytes 196616 | tf_op jit(solution)/shard_map/ppermute | solution.py:497
  70.5 4.8 %collective-permute-start.9 = (bf16[2,512,128]{2,1,0:T(8,128)(2,1)S(1)}, bf16[2,512,128]{2,1,0:T(8,128)(2,1)S(1)}, u32[]{:S(2)}, u32[]{:S(2)}) collective-permute-start(bf16[2,512,128]{2,1,0:T(8,128)(2,1)S(1)} %get-tuple-element.42), channel_id=1, source_target_pairs={{0,16},{16,0},{32,48},{48,32},{64,80},{80,64},{96,112},{112,96},{1... | collective-permute-start | bytes 786440 | tf_op jit(solution)/shard_map/ppermute | solution.py:497
